TPU v7x, 32 devices: a whole 2x2x4 slice. The times are simulated.
32 devices in a mesh: dp: 4 (over y, x), ctx: 8 (over z, core).
Axes of the slice: x: 2, y: 2, z: 4, core: 2. Of those that a mesh axis runs over, the one named last changes fastest.
Arguments:
- inputs: bfloat16 [4, 64, 8192], P('dp', None, 'ctx'), may hold values from -6 to 6
- cotangent: bfloat16 [4, 64, 8192], P('dp', None, 'ctx'), may hold values from -6 to 6
- filters: float32 [64, 8192], P(None, 'ctx'), may hold values from -6 to 6
- skip_gain: float32 [64], replicated, may hold values from 0.1 to 1.9
Outputs:
- input_grad: bfloat16 [4, 64, 8192], P('dp', None, 'ctx')
- filter_grad: float32 [64, 8192], P(None, 'ctx')
All inputs are finite; a program needn't handle non-finite values.
Results may differ from a plain program's by a relative error of at most 0.001.
Values sent between devices are 32-bit elements; how exact they have to be, the bound alone decides.
A program may use at most 128 MiB of HBM per device.

v0:
```python
import math

import jax
import jax.numpy as jnp
from jax import lax
from jax.sharding import PartitionSpec as P


def from_partner(x, axis, stride):
    return lax.ppermute(x, axis, [(i, i ^ 1 << stride) for i in range(lax.axis_size(axis))])


def product(left_side, right_side):
    return jnp.dot(
        left_side, right_side, precision=lax.Precision.HIGHEST, preferred_element_type=jnp.float32
    )


def complex_mul(values, cosine, sine_part):
    real_out = values[0] * cosine - values[1] * sine_part
    imag_out = values[0] * sine_part + values[1] * cosine
    return jnp.stack([real_out, imag_out])


def square_tables(count):
    position = jnp.arange(count, dtype=jnp.int32)
    phase_int = position[:, None] * position[None, :] % count
    angles = 2.0 * math.pi / count * phase_int.astype(jnp.float32)
    return (jnp.cos(angles), jnp.sin(angles))


def local_tables(length):
    outer_size = 2 ** ((length.bit_length() - 1) // 2)
    inner_size = length // outer_size
    outer_cos, outer_sin = square_tables(outer_size)
    inner_cos, inner_sin = square_tables(inner_size)
    outer_pos = jnp.arange(outer_size, dtype=jnp.int32)
    inner_pos = jnp.arange(inner_size, dtype=jnp.int32)
    phase_int = outer_pos[:, None] * inner_pos[None, :] % length
    angles = 2.0 * math.pi / length * phase_int.astype(jnp.float32)
    return (outer_cos, outer_sin, inner_cos, inner_sin, jnp.cos(angles), jnp.sin(angles))


def along_outer(real_rows, imag_rows, cos_table, sin_table, sign_value):
    highest = lax.Precision.HIGHEST

    def contract(table, rows):
        return jnp.einsum("ka,rab->rkb", table, rows, precision=highest)

    real_out = contract(cos_table, real_rows) - sign_value * contract(sin_table, imag_rows)
    imag_out = contract(cos_table, imag_rows) + sign_value * contract(sin_table, real_rows)
    return (real_out, imag_out)


def along_inner(real_rows, imag_rows, cos_table, sin_table, sign_value):
    row_shape = real_rows.shape
    inner_size = row_shape[-1]
    flat_real = real_rows.reshape(-1, inner_size)
    flat_imag = imag_rows.reshape(-1, inner_size)
    real_out = product(flat_real, cos_table) - sign_value * product(flat_imag, sin_table)
    imag_out = product(flat_imag, cos_table) + sign_value * product(flat_real, sin_table)
    return (real_out.reshape(row_shape), imag_out.reshape(row_shape))


def local_dft(values, tables, inverse):
    outer_cos, outer_sin, inner_cos, inner_sin, twist_cos, twist_sin = tables
    outer_size = outer_cos.shape[0]
    inner_size = inner_cos.shape[0]
    row_shape = values.shape[1:]
    length = row_shape[-1]
    real_rows = values[0].reshape(-1, outer_size, inner_size)
    imag_rows = values[1].reshape(-1, outer_size, inner_size)
    if inverse:
        real_rows, imag_rows = along_inner(real_rows, imag_rows, inner_cos, inner_sin, 1.0)
        turned = complex_mul(jnp.stack([real_rows, imag_rows]), twist_cos, twist_sin)
        real_rows, imag_rows = along_outer(turned[0], turned[1], outer_cos, outer_sin, 1.0)
        real_rows = real_rows / length
        imag_rows = imag_rows / length
    else:
        real_rows, imag_rows = along_outer(real_rows, imag_rows, outer_cos, outer_sin, -1.0)
        turned = complex_mul(jnp.stack([real_rows, imag_rows]), twist_cos, -twist_sin)
        real_rows, imag_rows = along_inner(turned[0], turned[1], inner_cos, inner_sin, -1.0)
    return jnp.stack([real_rows.reshape(row_shape), imag_rows.reshape(row_shape)])


def cross_forward(values):
    devices = lax.axis_size("ctx")
    device = lax.axis_index("ctx")
    sections = devices.bit_length() - 1
    freq_index = jnp.zeros((), jnp.int32)
    for section_bit in reversed(range(sections)):
        half_width = 1 << section_bit
        is_upper = device >> section_bit & 1 == 1
        partner = from_partner(values, "ctx", section_bit)
        offset = (device % half_width).astype(jnp.float32)
        angles = -math.pi * offset / half_width
        twisted = complex_mul(partner - values, jnp.cos(angles), jnp.sin(angles))
        values = jnp.where(is_upper, twisted, values + partner)
    for section_bit in range(sections):
        freq_index = freq_index + ((device >> section_bit & 1) << sections - 1 - section_bit)
    return (values, freq_index)


def cross_inverse(values):
    devices = lax.axis_size("ctx")
    device = lax.axis_index("ctx")
    sections = devices.bit_length() - 1
    for section_bit in range(sections):
        half_width = 1 << section_bit
        is_upper = device >> section_bit & 1 == 1
        offset = (device % half_width).astype(jnp.float32)
        angles = math.pi * offset / half_width
        sent = jnp.where(is_upper, complex_mul(values, jnp.cos(angles), jnp.sin(angles)), values)
        partner = from_partner(sent, "ctx", section_bit)
        values = jnp.where(is_upper, partner - sent, partner + sent) * 0.5
    return values


def twiddle(values, freq_index, padded_length, direction):
    length = values.shape[-1]
    position = jnp.arange(length, dtype=jnp.int32)
    parity = jnp.arange(2, dtype=jnp.int32)
    phase_int = position[None, :] * (2 * freq_index + parity[:, None]) % padded_length
    angles = direction * 2.0 * math.pi / padded_length * phase_int.astype(jnp.float32)
    return complex_mul(values, jnp.cos(angles)[:, None, :], jnp.sin(angles)[:, None, :])


def forward_transform(signal_real, signal_imag, tables):
    devices = lax.axis_size("ctx")
    device = lax.axis_index("ctx")
    padded_length = 2 * devices * signal_real.shape[-1]
    angles = -math.pi * device.astype(jnp.float32) / devices
    cosine = jnp.cos(angles)
    sine_part = jnp.sin(angles)
    odd_real = signal_real * cosine - signal_imag * sine_part
    odd_imag = signal_real * sine_part + signal_imag * cosine
    values = jnp.stack([jnp.stack([signal_real, odd_real]), jnp.stack([signal_imag, odd_imag])])
    values, freq_index = cross_forward(values)
    values = twiddle(values, freq_index, padded_length, -1.0)
    return (local_dft(values, tables, False), freq_index)


def inverse_transform(values, freq_index, tables):
    devices = lax.axis_size("ctx")
    device = lax.axis_index("ctx")
    padded_length = 2 * devices * values.shape[-1]
    values = local_dft(values, tables, True)
    values = twiddle(values, freq_index, padded_length, 1.0)
    values = cross_inverse(values)
    angles = math.pi * device.astype(jnp.float32) / devices
    cosine = jnp.cos(angles)
    sine_part = jnp.sin(angles)
    real_part = 0.5 * (values[0, 0] + values[0, 1] * cosine - values[1, 1] * sine_part)
    imag_part = 0.5 * (values[1, 0] + values[0, 1] * sine_part + values[1, 1] * cosine)
    return (real_part, imag_part)


def conj_product(first_spec, second_spec, factor):
    real_out = first_spec[0] * second_spec[0] + first_spec[1] * second_spec[1]
    imag_out = first_spec[0] * second_spec[1] - first_spec[1] * second_spec[0]
    return jnp.stack([real_out, imag_out]) * factor


def body(inputs, cotangent, filters, skip_gain):
    channels = filters.shape[0]
    length = filters.shape[1]
    factor = 1.0 / math.sqrt(lax.axis_size("ctx") * length)
    grad_rows = cotangent[0].astype(jnp.float32)
    input_rows = inputs[0].astype(jnp.float32)
    tables = local_tables(length)
    stacked = jnp.concatenate([grad_rows, input_rows, filters], axis=0)
    spectra, freq_index = forward_transform(stacked, jnp.zeros_like(stacked), tables)
    grad_spec = spectra[:, :, :channels]
    input_spec = spectra[:, :, channels : 2 * channels]
    filter_spec = spectra[:, :, 2 * channels :]
    through, unused_part = inverse_transform(
        conj_product(filter_spec, grad_spec, factor), freq_index, tables
    )
    filter_term = conj_product(input_spec, grad_spec, factor)
    summed = lax.psum(filter_term, "dp")
    filter_grad, unused_rest = inverse_transform(summed, freq_index, tables)
    input_grad = (through + skip_gain[:, None] * grad_rows).astype(jnp.bfloat16)[None]
    return (input_grad, filter_grad)


def solution(mesh):
    return jax.shard_map(
        body,
        mesh=mesh,
        in_specs=(P("dp", None, "ctx"), P("dp", None, "ctx"), P(None, "ctx"), P()),
        out_specs=(P("dp", None, "ctx"), P(None, "ctx")),
        check_vma=False,
    )
```

profile of v0, /device:TPU:0, one launch (start us, length us, event | category | flops | bytes accessed | tf_op | source)
XLA Modules:
  0.0 605.4 jit_solution(13697900731809366147)
XLA Ops:
  10.9 1.8 pad_maximum_fusion
  12.7 4.0 collective-permute-start
  16.9 135.7 %collective-permute-done = f32[2,2,192,1024]{3,2,1,0:T(8,128)} collective-permute-done((f32[2,2,192,1024]{3,2,1,0:T(8,128)}, f32[2,2,192,1024]{3,2,1,0:T(8,128)}, u32[]{:S(2)}, u32[]{:S(2)}) %collective-permute-start) | collective-permute-done | bytes 3145760 | tf_op jit(solution)/shard_map/ppermute | solution.py:10
  152.6 2.6 fusion.184
  155.6 5.7 maximum_select_fusion
  162.2 68.7 %collective-permute-done.1 = f32[2,2,192,1024]{3,2,1,0:T(8,128)} collective-permute-done((f32[2,2,192,1024]{3,2,1,0:T(8,128)}, f32[2,2,192,1024]{3,2,1,0:T(8,128)}, u32[]{:S(2)}, u32[]{:S(2)}) %collective-permute-start.1) | collective-permute-done | bytes 3145760 | tf_op jit(solution)/shard_map/ppermute | solution.py:10
  231.0 5.2 fusion.200
  238.0 5.1 maximum_select_fusion.1
  244.5 3.2 mul.1135
  247.7 3.7 mul.1136
  252.5 3.2 mul.1138
  255.7 3.8 mul.1139
  260.0 2.6 sub.185
  263.0 3.0 maximum_select_fusion.2
  265.9 1.9 fusion.185
  267.8 2.7 copy.113
  270.5 2.8 squeeze.4
  273.4 3.2 copy.115
  276.5 2.8 squeeze.5
  279.3 3.6 multiply_subtract_fusion.3
  282.9 2.5 fusion.6
  285.4 2.5 fusion.2
  287.9 2.6 multiply_subtract_fusion.2
  290.5 3.2 fusion.1
  293.7 4.0 copy.124
  297.7 4.7 reshape_squeeze_stack.9
  302.4 2.7 convolution_multiply_fusion.1
  305.2 4.0 copy.123
  309.2 4.7 reshape_squeeze_stack.8
  313.9 2.8 convolution_multiply_fusion
  316.7 2.7 convolution_subtract_fusion
  319.4 5.0 copy.125
  324.4 6.0 stack_reshape_reshape.6
  330.5 2.8 convolution_add_fusion
  333.2 5.0 copy.126
  338.3 5.4 stack_reshape_reshape.7
  345.8 2.4 fusion.68
  348.3 2.0 reshape_reshape_squeeze.13
  350.3 4.1 fusion.66
  354.5 3.2 convolution_subtract_fusion.2
  359.4 4.8 convolution_add_fusion.2
  364.1 3.2 squeeze_stack_reshape.33
  368.4 4.7 fusion.16
  373.1 2.6 fusion.9
  379.7 4.3 fusion.17
  384.0 2.6 fusion.11
  388.9 34.3 %all-reduce.3.cloned.1.call-done = f32[2,2,64,1024]{3,2,1,0:T(8,128)} async-done(((f32[2,2,64,1024]{3,2,1,0:T(8,128)}), f32[2,2,64,1024]{3,2,1,0:T(8,128)}) %all-reduce.3.cloned.1.call-update) | async-done | bytes 1048592 | tf_op jit(solution)/shard_map/psum | solution.py:180
  425.2 2.4 fusion.64
  427.6 2.0 reshape_reshape_squeeze.15
  429.6 4.1 fusion.72
  433.8 3.2 convolution_subtract_fusion.1
  438.7 4.0 convolution_add_fusion.1
  442.7 2.0 squeeze_stack_reshape.37
  444.7 4.3 fusion.18
  449.0 3.6 fusion.19
  452.6 2.6 fusion.13
  459.1 4.2 fusion.15
  471.1 1.8 select_multiply_fusion.2
  480.4 20.2 %collective-permute-done.7 = f32[2,2,64,1024]{3,2,1,0:T(8,128)} collective-permute-done((f32[2,2,64,1024]{3,2,1,0:T(8,128)}, f32[2,2,64,1024]{3,2,1,0:T(8,128)}, u32[]{:S(2)}, u32[]{:S(2)}) %collective-permute-start.7) | collective-permute-done | bytes 1048608 | tf_op jit(solution)/shard_map/ppermute | solution.py:10
  500.6 1.8 select_multiply_fusion.1
  503.7 2.4 collective-permute-start.8
  506.1 34.2 %collective-permute-done.4 = f32[2,2,64,1024]{3,2,1,0:T(8,128)} collective-permute-done((f32[2,2,64,1024]{3,2,1,0:T(8,128)}, f32[2,2,64,1024]{3,2,1,0:T(8,128)}, u32[]{:S(2)}, u32[]{:S(2)}) %collective-permute-start.4) | collective-permute-done | bytes 1048608 | tf_op jit(solution)/shard_map/ppermute | solution.py:10
  544.2 31.8 %collective-permute-done.8 = f32[2,2,64,1024]{3,2,1,0:T(8,128)} collective-permute-done((f32[2,2,64,1024]{3,2,1,0:T(8,128)}, f32[2,2,64,1024]{3,2,1,0:T(8,128)}, u32[]{:S(2)}, u32[]{:S(2)}) %collective-permute-start.8) | collective-permute-done | bytes 1048608 | tf_op jit(solution)/shard_map/ppermute | solution.py:10
  578.3 17.7 %collective-permute-done.5 = f32[2,2,64,1024]{3,2,1,0:T(8,128)} collective-permute-done((f32[2,2,64,1024]{3,2,1,0:T(8,128)}, f32[2,2,64,1024]{3,2,1,0:T(8,128)}, u32[]{:S(2)}, u32[]{:S(2)}) %collective-permute-start.5) | collective-permute-done | bytes 1048608 | tf_op jit(solution)/shard_map/ppermute | solution.py:10
  (148 shorter events, 52.9 us)
Async XLA Ops:
  7.2 3.1 copy-start.36
  7.2 416.0 %all-reduce.3.cloned.1.call-start = ((), (), s32[]{:S(2)}) async-start(), calls=%async_computation | async-start | bytes 2097152 | tf_op jit(solution)/shard_map/psum | solution.py:180
  12.7 139.9 %collective-permute-start = (f32[2,2,192,1024]{3,2,1,0:T(8,128)}, f32[2,2,192,1024]{3,2,1,0:T(8,128)}, u32[]{:S(2)}, u32[]{:S(2)}) collective-permute-start(f32[2,2,192,1024]{3,2,1,0:T(8,128)} %pad_maximum_fusion), channel_id=1, source_target_pairs={{0,4},{1,5},{2,6},{3,7},{4,0},{5,1},{6,2},{7,3},{8,12},{9,13},{10,... | collective-permute-start | bytes 9437192 | tf_op jit(solution)/shard_map/ppermute | solution.py:10
  155.6 5.8 copy-start.3
  155.6 5.8 copy-start.5
  161.3 69.6 %collective-permute-start.1 = (f32[2,2,192,1024]{3,2,1,0:T(8,128)}, f32[2,2,192,1024]{3,2,1,0:T(8,128)}, u32[]{:S(2)}, u32[]{:S(2)}) collective-permute-start(f32[2,2,192,1024]{3,2,1,0:T(8,128)} %maximum_select_fusion), channel_id=1, source_target_pairs={{0,2},{1,3},{2,0},{3,1},{4,6},{5,7},{6,4},{7,5},{8,10},{9,11},{10,... | collective-permute-start | bytes 9437192 | tf_op jit(solution)/shard_map/ppermute | solution.py:10
  236.2 1.4 copy-start.4
  236.2 1.9 copy-start.6
  243.2 16.9 %collective-permute-start.2 = (f32[2,2,192,1024]{3,2,1,0:T(8,128)}, f32[2,2,192,1024]{3,2,1,0:T(8,128)S(1)}, u32[]{:S(2)}, u32[]{:S(2)}) collective-permute-start(f32[2,2,192,1024]{3,2,1,0:T(8,128)} %maximum_select_fusion.1), channel_id=1, source_target_pairs={{0,1},{1,0},{2,3},{3,2},{4,5},{5,4},{6,7},{7,6},{8,9},{9,8},{10,11... | collective-permute-start | bytes 9437192 | tf_op jit(solution)/shard_map/ppermute | solution.py:10
  313.9 2.8 copy-start.12
  324.4 6.0 copy-start.11
  338.3 5.4 copy-start.13
  345.8 4.5 copy-start.7
  350.3 4.1 copy-start.9
  364.1 3.2 copy-start.34
  364.1 3.2 copy-start.35
  368.4 4.7 copy-start
  379.7 4.3 copy-start.1
  425.1 4.5 copy-start.8
  429.6 4.1 copy-start.10
  444.7 4.3 copy-start.2
  467.5 0.8 copy-start.18
  467.5 1.2 copy-start.14
  467.6 0.9 copy-start.19
  468.3 2.8 collective-permute-start.6
  468.6 1.3 copy-start.16
  469.8 5.9 collective-permute-start.3
  473.1 2.6 copy-start.20
  473.1 2.6 copy-start.21
  473.1 2.6 copy-start.15
  473.1 2.6 copy-start.17
  474.2 26.3 %collective-permute-start.7 = (f32[2,2,64,1024]{3,2,1,0:T(8,128)}, f32[2,2,64,1024]{3,2,1,0:T(8,128)}, u32[]{:S(2)}, u32[]{:S(2)}) collective-permute-start(f32[2,2,64,1024]{3,2,1,0:T(8,128)} %maximum_select_fusion.7), channel_id=1, source_target_pairs={{0,2},{1,3},{2,0},{3,1},{4,6},{5,7},{6,4},{7,5},{8,10},{9,11},{10,... | collective-permute-start | bytes 3145736 | tf_op jit(solution)/shard_map/ppermute | solution.py:10
  477.5 0.8 copy-start.22
  477.5 1.9 copy-start.24
  479.4 60.9 %collective-permute-start.4 = (f32[2,2,64,1024]{3,2,1,0:T(8,128)}, f32[2,2,64,1024]{3,2,1,0:T(8,128)}, u32[]{:S(2)}, u32[]{:S(2)}) collective-permute-start(f32[2,2,64,1024]{3,2,1,0:T(8,128)} %maximum_select_fusion.4), channel_id=1, source_target_pairs={{0,2},{1,3},{2,0},{3,1},{4,6},{5,7},{6,4},{7,5},{8,10},{9,11},{10,... | collective-permute-start | bytes 3145736 | tf_op jit(solution)/shard_map/ppermute | solution.py:10
  502.6 3.6 copy-start.26
  502.6 3.6 copy-start.28
  502.6 37.7 %copy-start.23 = (f32[1,2,64,1024]{3,2,1,0:T(8,128)S(1)}, f32[1,2,64,1024]{3,2,1,0:T(8,128)}, u32[]{:S(2)}) copy-start(f32[1,2,64,1024]{3,2,1,0:T(8,128)} %copy-done.22) | copy-start | bytes 1572868
  502.6 37.7 %copy-start.25 = (f32[1,2,64,1024]{3,2,1,0:T(8,128)S(1)}, f32[1,2,64,1024]{3,2,1,0:T(8,128)}, u32[]{:S(2)}) copy-start(f32[1,2,64,1024]{3,2,1,0:T(8,128)} %copy-done.24) | copy-start | bytes 1572868
  503.7 72.3 %collective-permute-start.8 = (f32[2,2,64,1024]{3,2,1,0:T(8,128)}, f32[2,2,64,1024]{3,2,1,0:T(8,128)}, u32[]{:S(2)}, u32[]{:S(2)}) collective-permute-start(f32[2,2,64,1024]{3,2,1,0:T(8,128)} %maximum_select_fusion.8), channel_id=1, source_target_pairs={{0,4},{1,5},{2,6},{3,7},{4,0},{5,1},{6,2},{7,3},{8,12},{9,13},{10,... | collective-permute-start | bytes 3145736 | tf_op jit(solution)/shard_map/ppermute | solution.py:10
  542.1 0.8 copy-start.30
  542.1 1.9 copy-start.32
  542.1 33.9 %copy-start.27 = (f32[1,2,64,1024]{3,2,1,0:T(8,128)S(1)}, f32[1,2,64,1024]{3,2,1,0:T(8,128)}, u32[]{:S(2)}) copy-start(f32[1,2,64,1024]{3,2,1,0:T(8,128)} %copy-done.26) | copy-start | bytes 1572868
  542.1 33.9 %copy-start.29 = (f32[1,2,64,1024]{3,2,1,0:T(8,128)S(1)}, f32[1,2,64,1024]{3,2,1,0:T(8,128)}, u32[]{:S(2)}) copy-start(f32[1,2,64,1024]{3,2,1,0:T(8,128)} %copy-done.28) | copy-start | bytes 1572868
  544.0 52.0 %collective-permute-start.5 = (f32[2,2,64,1024]{3,2,1,0:T(8,128)}, f32[2,2,64,1024]{3,2,1,0:T(8,128)}, u32[]{:S(2)}, u32[]{:S(2)}) collective-permute-start(f32[2,2,64,1024]{3,2,1,0:T(8,128)} %maximum_select_fusion.5), channel_id=1, source_target_pairs={{0,4},{1,5},{2,6},{3,7},{4,0},{5,1},{6,2},{7,3},{8,12},{9,13},{10,... | collective-permute-start | bytes 3145736 | tf_op jit(solution)/shard_map/ppermute | solution.py:10
  544.2 51.8 %copy-start.31 = (f32[1,2,64,1024]{3,2,1,0:T(8,128)S(1)}, f32[1,2,64,1024]{3,2,1,0:T(8,128)}, u32[]{:S(2)}) copy-start(f32[1,2,64,1024]{3,2,1,0:T(8,128)} %copy-done.30) | copy-start | bytes 1572868
  544.2 51.8 %copy-start.33 = (f32[1,2,64,1024]{3,2,1,0:T(8,128)S(1)}, f32[1,2,64,1024]{3,2,1,0:T(8,128)}, u32[]{:S(2)}) copy-start(f32[1,2,64,1024]{3,2,1,0:T(8,128)} %copy-done.32) | copy-start | bytes 1572868
  578.3 19.3 %copy-start.37 = (bf16[1,64,1024]{2,1,0:T(8,128)(2,1)S(1)}, bf16[1,64,1024]{2,1,0:T(8,128)(2,1)}, u32[]{:S(2)}) copy-start(bf16[1,64,1024]{2,1,0:T(8,128)(2,1)} %param.5) | copy-start | bytes 393220
  578.3 19.3 %copy-start.38 = (f32[64]{0:T(128)S(1)}, f32[64]{0:T(128)}, u32[]{:S(2)}) copy-start(f32[64]{0:T(128)} %param.7) | copy-start | bytes 772
Sparse Core Ops, SparseCore 0:
  368.5 54.6 all-reduce.2
where the time goes:
time: 611 us; the launch traced here: 605 us
  waiting for transfers between devices  343 us (56%)
  local copies, waits for them, and re-layouts  100 us (16%)
  matrix products  78.7 us (13%)
  other arithmetic  57.2 us (9%)
  between operations  16.1 us (3%)
  starting transfers between devices  9.7 us (2%)
    ppermute x9, waiting for transfers between devices, from_partner(): lax.ppermute(x, axis, [(i, i ^ 1 << stride) for i in range(lax.axis_size(...  309 us
    dot_general x12, matrix products, contract(): return jnp.einsum('ka,rab->rkb', table, rows, precision=highest)  39.6 us
    dot_general x12, matrix products, product(): jnp.dot(left_side, right_side, precision=lax.Precision.HIGHEST, preferred...  39.2 us
    psum x1, waiting for transfers between devices, body(): summed = lax.psum(filter_term, 'dp')  34.3 us
    another operation x12, local copies, waits for them, and re-layouts, complex_mul(): real_out = values[0] * cosine - values[1] * sine_part  18.2 us
    mul x4, local copies, waits for them, and re-layouts, complex_mul(): real_out = values[0] * cosine - values[1] * sine_part  13.9 us
    select_n x3, other arithmetic, cross_forward(): values = jnp.where(is_upper, twisted, values + partner)  13.8 us
  transfers between devices with their start and end apart: 10, of which 8 were waited for; matrix products, arithmetic and copies ran while one was open for 9% of the time, Pallas kernels for 0%

commit v1 on v0

v1 whole, which is shorter than its diff:
```python
import functools
import math

import jax
import jax.numpy as jnp
import ml_dtypes
import numpy as np
from jax import lax
from jax.experimental import pallas as pl
from jax.experimental.pallas import tpu as pltpu
from jax.sharding import PartitionSpec as P

LANES = 128
MESH = pl.DeviceIdType.MESH


def dft_tables(length):
    half = length // LANES
    row = np.arange(half)
    lane = np.arange(LANES)
    theta = 2 * math.pi / (2 * half) * (((row[:, None] + 0.5) * row[None, :]) % (2 * half))
    outer = np.concatenate([np.cos(theta), -np.sin(theta)])
    phi = math.pi / length * ((row[:, None] + 0.5) * lane[None, :])
    phi_table = np.stack([np.cos(phi), -np.sin(phi)])
    psi = 2 * math.pi / LANES * ((lane[:, None] * lane[None, :]) % LANES)
    cos, sin = np.cos(psi), np.sin(psi)
    inner = np.block([[cos, -sin], [sin, cos]])
    back = outer.T / length / math.sqrt(length)
    return outer, phi_table.astype(np.float32), inner, back


def np_split(table):
    high = table.astype(ml_dtypes.bfloat16)
    low = (table - high.astype(np.float64)).astype(ml_dtypes.bfloat16)
    return high, low


def split(values):
    high = values.astype(jnp.bfloat16)
    return high, (values - high.astype(jnp.float32)).astype(jnp.bfloat16)


def dot(left, right):
    return jnp.dot(left, right, preferred_element_type=jnp.float32)


def plain_gradients(grads, inputs, filters):
    batch, channels, length = grads.shape
    half = length // LANES
    outer, phi, inner, back = dft_tables(length)
    outer, inner, back = (t.astype(np.float32) for t in (outer, inner, back))
    product = functools.partial(jnp.matmul, precision=lax.Precision.HIGHEST)

    def forward(values):
        rows = product(outer, values.reshape(values.shape[:-1] + (half, LANES)))
        real, imag = rows[..., :half, :], rows[..., half:, :]
        turned = jnp.concatenate(
            [real * phi[0] - imag * phi[1], real * phi[1] + imag * phi[0]], axis=-1
        )
        spec = product(turned, inner)
        return spec[..., :LANES], spec[..., LANES:]

    def backward(real, imag):
        rows = product(jnp.concatenate([real, imag], axis=-1), inner.T)
        real, imag = rows[..., :LANES], rows[..., LANES:]
        turned = jnp.concatenate(
            [real * phi[0] + imag * phi[1], imag * phi[0] - real * phi[1]], axis=-2
        )
        out = product(back, turned)
        return out.reshape(out.shape[:-2] + (length,))

    def conj_product(first, second):
        return (
            first[0] * second[0] + first[1] * second[1],
            first[0] * second[1] - first[1] * second[0],
        )

    grad_spec = forward(grads)
    through = backward(*conj_product(forward(filters), grad_spec))
    real, imag = conj_product(forward(inputs), grad_spec)
    return through, backward(real.sum(0), imag.sum(0))


def plain_body(inputs, cotangent, filters, skip_gain):
    def gather(values):
        return lax.all_to_all(values, "ctx", 0, 1, tiled=True)

    grad_rows = cotangent[0].astype(jnp.float32)
    grads, rows = gather(grad_rows), gather(inputs[0].astype(jnp.float32))
    through, filter_grad = plain_gradients(grads[None], rows[None], gather(filters))
    filter_grad = lax.psum(filter_grad, "dp")
    through = lax.all_to_all(through[0], "ctx", 1, 0, tiled=True)
    filter_grad = lax.all_to_all(filter_grad, "ctx", 1, 0, tiled=True)
    return (through + skip_gain[:, None] * grad_rows).astype(jnp.bfloat16)[None], filter_grad


def kernel(
    groups, parts, count, half,
    x_ref, g_ref, f_ref, outer_ref, outer3_ref, phi_ref, inner_ref, inner_t_ref, back_ref,
    out_ref,
    send_gx, send_f, recv_gx, recv_f, send_out,
    gx_send, gx_recv, f_send, f_recv, out_send, out_recv,
):
    devices = groups * parts
    rows = x_ref.shape[2] // LANES
    group, part = lax.axis_index("dp"), lax.axis_index("ctx")
    me = group * parts + part

    barrier = pltpu.get_barrier_semaphore()

    @pl.loop(1, devices)
    def _(step):
        other = lax.rem(me + step, devices)
        pl.semaphore_signal(
            barrier, inc=1, device_id=(other // parts, lax.rem(other, parts)),
            device_id_type=MESH,
        )

    for i in range(count):
        own = slice(i * devices, (i + 1) * devices)
        for r in range(rows):
            lanes = slice(r * LANES, (r + 1) * LANES)
            send_gx[i, :, 0, r, :] = g_ref[0, own, lanes].astype(jnp.float32)
            send_gx[i, :, 1, r, :] = x_ref[0, own, lanes].astype(jnp.float32)
            send_f[i, :, r, :] = f_ref[own, lanes]

    pl.semaphore_wait(barrier, devices - 1)

    def filter_copy(i, step, to):
        other = lax.rem(part + step, parts) if to else lax.rem(part - step + parts, parts)
        return pltpu.make_async_remote_copy(
            src_ref=send_f.at[i, group * parts + other],
            dst_ref=recv_f.at[i, part if to else other],
            send_sem=f_send.at[i, step],
            recv_sem=f_recv.at[i, step],
            device_id=(group, other),
            device_id_type=MESH,
        )

    def row_copy(i, step, to):
        lead, rest = step // parts, lax.rem(step, parts)
        if to:
            there = (lax.rem(group + lead, groups), lax.rem(part + rest, parts))
            slot = (group, part)
        else:
            there = (lax.rem(group - lead + groups, groups), lax.rem(part - rest + parts, parts))
            slot = there
        return pltpu.make_async_remote_copy(
            src_ref=send_gx.at[i, there[0] * parts + there[1]],
            dst_ref=recv_gx.at[i, slot[0], slot[1]],
            send_sem=gx_send.at[i, step],
            recv_sem=gx_recv.at[i, step],
            device_id=there,
            device_id_type=MESH,
        )

    def out_copy(i, step, to):
        lead, rest = step // parts, lax.rem(step, parts)
        if to:
            there = (lax.rem(group + lead, groups), lax.rem(part + rest, parts))
            channel = i * devices + me
        else:
            there = (lax.rem(group - lead + groups, groups), lax.rem(part - rest + parts, parts))
            channel = i * devices + there[0] * parts + there[1]
        return pltpu.make_async_remote_copy(
            src_ref=send_out.at[i, there[0], there[1]],
            dst_ref=out_ref.at[channel],
            send_sem=out_send.at[i, step],
            recv_sem=out_recv.at[i, step],
            device_id=there,
            device_id_type=MESH,
        )

    for i in range(count):
        pl.loop(1, parts)(lambda step: filter_copy(i, step, True).start())
        pl.loop(1, devices)(lambda step: row_copy(i, step, True).start())
    for i in range(count):
        recv_gx[i, group, part] = send_gx[i, me]
        recv_f[i, part] = send_f[i, me]

    def product3(left, right):
        (left_high, left_low), (right_high, right_low) = left, right
        return (
            dot(left_high, right_high) + dot(left_low, right_high) + dot(left_high, right_low)
        )

    def turn(real, imag, sine):
        cosine = phi_ref[0]
        return real * cosine - imag * sine, real * sine + imag * cosine

    for i in range(count):
        pl.loop(1, parts)(lambda step: filter_copy(i, step, False).wait_recv())
        pl.loop(1, devices)(lambda step: row_copy(i, step, False).wait_recv())

        def signal(kind, b):
            return recv_gx[i, b, :, kind].reshape(half, LANES).astype(jnp.bfloat16)

        exact = jnp.concatenate(
            [signal(0, b) for b in range(groups)] + [signal(1, b) for b in range(groups)], axis=1
        )
        high, low = split(recv_f[i].reshape(half, LANES))
        stepped = dot(outer_ref[...], jnp.concatenate([exact, exact], axis=0))
        filter_part = dot(outer3_ref[...], jnp.concatenate([high, high, low], axis=0))
        stepped = jnp.concatenate([stepped, filter_part], axis=1)
        turned = []
        for s in range(2 * groups + 1):
            lanes = slice(s * LANES, (s + 1) * LANES)
            pair = turn(stepped[:half, lanes], stepped[half:, lanes], phi_ref[1])
            turned.append(jnp.concatenate(pair, axis=1))
        spec = product3(split(jnp.concatenate(turned, axis=0)), (inner_ref[0], inner_ref[1]))

        def piece(s):
            block = spec[s * half:(s + 1) * half]
            return block[:, :LANES], block[:, LANES:]

        filter_spec = piece(2 * groups)
        products = []
        total = None
        for b in range(groups):
            grad_spec, input_spec = piece(b), piece(groups + b)
            for first in (filter_spec, input_spec):
                term = jnp.concatenate(
                    [
                        first[0] * grad_spec[0] + first[1] * grad_spec[1],
                        first[0] * grad_spec[1] - first[1] * grad_spec[0],
                    ],
                    axis=1,
                )
                if first is filter_spec:
                    products.append(term)
                else:
                    total = term if total is None else total + term
        products.append(total)
        folded = product3(split(jnp.concatenate(products, axis=0)), (inner_t_ref[0], inner_t_ref[1]))
        turned = []
        for s in range(groups + 1):
            block = folded[s * half:(s + 1) * half]
            pair = turn(block[:, :LANES], block[:, LANES:], -phi_ref[1])
            turned.append(jnp.concatenate(pair, axis=0))
        final = product3((back_ref[0], back_ref[1]), split(jnp.concatenate(turned, axis=1)))
        filter_grad = final[:, groups * LANES:].reshape(parts, rows, LANES)
        for b in range(groups):
            through = final[:, b * LANES:(b + 1) * LANES]
            send_out[i, b, :, 0] = through.reshape(parts, rows, LANES)
            send_out[i, b, :, 1] = filter_grad
        pl.loop(1, devices)(lambda step: out_copy(i, step, True).start())
        out_ref[i * devices + me] = send_out[i, group, part]

    for i in range(count):
        pl.loop(1, parts)(lambda step: filter_copy(i, step, True).wait_send())
        pl.loop(1, devices)(lambda step: row_copy(i, step, True).wait_send())
        pl.loop(1, devices)(lambda step: out_copy(i, step, True).wait_send())
        pl.loop(1, devices)(lambda step: out_copy(i, step, False).wait_recv())


def fused_body(groups, parts, inputs, cotangent, filters, skip_gain):
    channels, width = filters.shape
    rows, half = width // LANES, parts * width // LANES
    devices = groups * parts
    count = channels // devices
    outer, phi, inner, back = dft_tables(parts * width)
    outer_high, outer_low = np_split(outer)
    tables = (
        np.concatenate([outer_high, outer_low], axis=1),
        np.concatenate([outer_high, outer_low, outer_high], axis=1),
        phi,
        np.stack(np_split(inner)),
        np.stack(np_split(inner.T)),
        np.stack(np_split(back)),
    )
    tile = (rows, LANES)
    out = pl.pallas_call(
        functools.partial(kernel, groups, parts, count, half),
        out_shape=jax.ShapeDtypeStruct((channels, 2) + tile, jnp.float32),
        in_specs=[pl.BlockSpec(memory_space=pltpu.VMEM)] * 9,
        out_specs=pl.BlockSpec(memory_space=pltpu.VMEM),
        scratch_shapes=[
            pltpu.VMEM((count, devices, 2) + tile, jnp.float32),
            pltpu.VMEM((count, devices) + tile, jnp.float32),
            pltpu.VMEM((count, groups, parts, 2) + tile, jnp.float32),
            pltpu.VMEM((count, parts) + tile, jnp.float32),
            pltpu.VMEM((count, groups, parts, 2) + tile, jnp.float32),
            pltpu.SemaphoreType.DMA((count, devices)),
            pltpu.SemaphoreType.DMA((count, devices)),
            pltpu.SemaphoreType.DMA((count, parts)),
            pltpu.SemaphoreType.DMA((count, parts)),
            pltpu.SemaphoreType.DMA((count, devices)),
            pltpu.SemaphoreType.DMA((count, devices)),
        ],
        compiler_params=pltpu.CompilerParams(
            collective_id=0, has_side_effects=True, vmem_limit_bytes=40 * 2**20
        ),
    )(inputs, cotangent, filters, *(jnp.asarray(t) for t in tables))
    through = out[:, 0].reshape(channels, width)
    input_grad = through + skip_gain[:, None] * cotangent[0].astype(jnp.float32)
    return input_grad.astype(jnp.bfloat16)[None], out[:, 1].reshape(channels, width)


def solution(mesh):
    groups, parts = mesh.shape["dp"], mesh.shape["ctx"]

    def body(inputs, cotangent, filters, skip_gain):
        if filters.shape[0] % (groups * parts) or inputs.shape[0] != 1:
            return plain_body(inputs, cotangent, filters, skip_gain)
        return fused_body(groups, parts, inputs, cotangent, filters, skip_gain)

    return jax.shard_map(
        body,
        mesh=mesh,
        in_specs=(P("dp", None, "ctx"), P("dp", None, "ctx"), P(None, "ctx"), P()),
        out_specs=(P("dp", None, "ctx"), P(None, "ctx")),
        check_vma=False,
    )
```

time: 611 us -> 46 us (0.08)
  waiting for transfers between devices: 343 us -> 0 us
  local copies, waits for them, and re-layouts: 100 us -> 9.53 us
  matrix products: 78.7 us -> 0 us
  other arithmetic: 57.2 us -> 0.75 us
  Pallas kernels: 0 us -> 34.6 us
  between operations: 16.1 us -> 0.67 us
  starting transfers between devices: 9.7 us -> 0 us
    ppermute x9 -> x0, waiting for transfers between devices: 309 us -> none  [from_partner(): lax.ppermute(x, axis, [(i, i ^ 1 << stride) for i in range(lax.axis_size(...]
    dot_general x24 -> x0, matrix products: 78.7 us -> none  [the longest x12 39.6 us: contract(): return jnp.einsum('ka,rab->rkb', table, rows, precision=highest)]
    another operation x20 -> x1, local copies, waits for them, and re-layouts: 44.6 us -> 0.05 us  [fused_body(): through = out[:, 0].reshape(channels, width)]
    pallas_call x0 -> x1, Pallas kernels: none -> 34.6 us  [fused_body(): pl.pallas_call(functools.partial(kernel, groups, parts, count, half), out...]
    psum x1 -> x0, waiting for transfers between devices: 34.3 us -> none  [body(): summed = lax.psum(filter_term, 'dp')]
    select_n x9 -> x0, other arithmetic: 19.6 us -> none  [the longest x3 13.8 us: cross_forward(): values = jnp.where(is_upper, twisted, values + partner)]
    sub x13 -> x0, other arithmetic: 17.8 us -> none  [the longest x3 10.3 us: cross_forward(): twisted = complex_mul(partner - values, jnp.cos(angles), jnp.sin(angles))]
    mul x4 -> x0, local copies, waits for them, and re-layouts: 13.9 us -> none  [complex_mul(): real_out = values[0] * cosine - values[1] * sine_part]
  transfers between devices with their start and end apart: 10 -> 0, of which waited for: 8 -> 0; matrix products, arithmetic and copies ran while one was open for 9% -> 0% of each run, Pallas kernels for 0% -> 0%
where the time goes in v1:
time: 46 us; the launch traced here: 45.5 us
  Pallas kernels  34.6 us (75%)
  local copies, waits for them, and re-layouts  9.53 us (21%)
  other arithmetic  0.75 us (2%)
  between operations  0.67 us (1%)
    pallas_call x1, Pallas kernels, fused_body(): pl.pallas_call(functools.partial(kernel, groups, parts, count, half), out...  34.6 us
    unnamed x23, local copies, waits for them, and re-layouts  9.45 us

profile of v1, /device:TPU:0, one launch (start us, length us, event | category | flops | bytes accessed | tf_op | source)
XLA Modules:
  0.0 45.5 jit_solution(1669117216906671993)
XLA Ops:
  0.6 0.0 copy-start
  0.6 0.9 %copy-done = bf16[1,64,1024]{2,1,0:T(8,128)(2,1)S(1)} copy-done((bf16[1,64,1024]{2,1,0:T(8,128)(2,1)S(1)}, bf16[1,64,1024]{2,1,0:T(8,128)(2,1)}, u32[]{:S(2)}) %copy-start) | copy-done | bytes 131096
  1.5 0.0 copy-start.2
  1.5 0.9 %copy-done.2 = f32[64,1024]{1,0:T(8,128)S(1)} copy-done((f32[64,1024]{1,0:T(8,128)S(1)}, f32[64,1024]{1,0:T(8,128)}, u32[]{:S(2)}) %copy-start.2) | copy-done | bytes 262168
  2.5 0.0 copy-start.3
  2.5 0.9 %copy-done.3 = bf16[2,256,256]{2,1,0:T(8,128)(2,1)S(1)} copy-done((bf16[2,256,256]{2,1,0:T(8,128)(2,1)S(1)}, bf16[2,256,256]{2,1,0:T(8,128)(2,1)}, u32[]{:S(2)}) %copy-start.3) | copy-done | bytes 262168
  3.4 0.0 copy-start.4
  3.4 0.9 %copy-done.4 = bf16[2,256,256]{2,1,0:T(8,128)(2,1)S(1)} copy-done((bf16[2,256,256]{2,1,0:T(8,128)(2,1)S(1)}, bf16[2,256,256]{2,1,0:T(8,128)(2,1)}, u32[]{:S(2)}) %copy-start.4) | copy-done | bytes 262168
  4.4 0.0 copy-start.5
  4.4 0.9 %copy-done.5 = bf16[1,64,1024]{2,1,0:T(8,128)(2,1)S(1)} copy-done((bf16[1,64,1024]{2,1,0:T(8,128)(2,1)S(1)}, bf16[1,64,1024]{2,1,0:T(8,128)(2,1)}, u32[]{:S(2)}) %copy-start.5) | copy-done | bytes 131096
  5.3 0.0 copy-start.6
  5.3 0.8 %copy-done.6 = f32[2,64,128]{2,1,0:T(8,128)S(1)} copy-done((f32[2,64,128]{2,1,0:T(8,128)S(1)}, f32[2,64,128]{2,1,0:T(8,128)}, u32[]{:S(2)}) %copy-start.6) | copy-done | bytes 65560
  6.1 0.0 copy-start.7
  6.1 0.8 %copy-done.7 = bf16[128,192]{1,0:T(8,128)(2,1)S(1)} copy-done((bf16[128,192]{1,0:T(8,128)(2,1)S(1)}, bf16[128,192]{1,0:T(8,128)(2,1)}, u32[]{:S(2)}) %copy-start.7) | copy-done | bytes 49176
  7.0 0.0 copy-start.8
  7.0 0.8 %copy-done.8 = bf16[2,64,128]{2,1,0:T(8,128)(2,1)S(1)} copy-done((bf16[2,64,128]{2,1,0:T(8,128)(2,1)S(1)}, bf16[2,64,128]{2,1,0:T(8,128)(2,1)}, u32[]{:S(2)}) %copy-start.8) | copy-done | bytes 32792
  7.7 0.0 copy-start.9
  7.7 0.8 %copy-done.9 = bf16[128,128]{1,0:T(8,128)(2,1)S(1)} copy-done((bf16[128,128]{1,0:T(8,128)(2,1)S(1)}, bf16[128,128]{1,0:T(8,128)(2,1)}, u32[]{:S(2)}) %copy-start.9) | copy-done | bytes 32792
  8.5 34.6 %shard_map.113 = f32[64,2,8,128]{3,2,1,0:T(8,128)S(1)} custom-call(bf16[1,64,1024]{2,1,0:T(8,128)(2,1)S(1)} %copy-done.5, bf16[1,64,1024]{2,1,0:T(8,128)(2,1)S(1)} %copy-done, f32[64,1024]{1,0:T(8,128)S(1)} %copy-done.2, bf16[128,128]{1,0:T(8,128)(2,1)S(1)} %copy-done.9, bf16[128,192]{1,0:T(8,128)(2,1)S(1)} %copy-done.7, f32[2,64,128]{2,1,0:T(8,128)S(1)} %copy-done.6, ...), custom_call_target="tpu_custom_call" | custom-call | tf_op jit(solution)/shard_map/pallas_call | solution.py:272
  43.1 0.8 %copy.14 = f32[8,8,8,128]{3,1,2,0:T(8,128)} copy(f32[8,8,8,128]{3,2,1,0:T(8,128)S(1)} %bitcast.7) | data formatting | bytes 524288
  43.8 0.0 copy-start.1
  43.8 0.0 copy-start.10
  43.9 0.9 %copy-done.1 = bf16[1,64,1024]{2,1,0:T(8,128)(2,1)S(1)} copy-done((bf16[1,64,1024]{2,1,0:T(8,128)(2,1)S(1)}, bf16[1,64,1024]{2,1,0:T(8,128)(2,1)}, u32[]{:S(2)}) %copy-start.1) | copy-done | bytes 131096
  44.7 0.0 copy-done.10
  44.8 0.8 %add_convert_fusion = bf16[1,64,1024]{2,1,0:T(8,128)(2,1)} fusion(f32[1,64,1024]{2,1,0:T(8,128)S(1)} %reshape_squeeze.6, bf16[1,64,1024]{2,1,0:T(8,128)(2,1)S(1)} %copy-done.1, f32[64]{0:T(128)S(1)} %copy-done.10), kind=kLoop, calls=%fused_computation.1 | loop fusion | flops 262144 | bytes 524544 | tf_op jit(solution)/shard_map/convert_element_type | solution.py:296
  (2 shorter events, 0.1 us)
Async XLA Ops:
  0.6 0.9 %copy-start = (bf16[1,64,1024]{2,1,0:T(8,128)(2,1)S(1)}, bf16[1,64,1024]{2,1,0:T(8,128)(2,1)}, u32[]{:S(2)}) copy-start(bf16[1,64,1024]{2,1,0:T(8,128)(2,1)} %g_ref.1) | copy-start | bytes 393220
  1.5 0.9 %copy-start.2 = (f32[64,1024]{1,0:T(8,128)S(1)}, f32[64,1024]{1,0:T(8,128)}, u32[]{:S(2)}) copy-start(f32[64,1024]{1,0:T(8,128)} %f_ref.1) | copy-start | bytes 786436
  2.5 0.9 %copy-start.3 = (bf16[2,256,256]{2,1,0:T(8,128)(2,1)S(1)}, bf16[2,256,256]{2,1,0:T(8,128)(2,1)}, u32[]{:S(2)}) copy-start(bf16[2,256,256]{2,1,0:T(8,128)(2,1)} %constant.16.clone.inner_t_ref) | copy-start | bytes 786436
  3.4 0.9 %copy-start.4 = (bf16[2,256,256]{2,1,0:T(8,128)(2,1)S(1)}, bf16[2,256,256]{2,1,0:T(8,128)(2,1)}, u32[]{:S(2)}) copy-start(bf16[2,256,256]{2,1,0:T(8,128)(2,1)} %constant.15.clone.inner_ref) | copy-start | bytes 786436
  4.4 0.9 %copy-start.5 = (bf16[1,64,1024]{2,1,0:T(8,128)(2,1)S(1)}, bf16[1,64,1024]{2,1,0:T(8,128)(2,1)}, u32[]{:S(2)}) copy-start(bf16[1,64,1024]{2,1,0:T(8,128)(2,1)} %x_ref.1) | copy-start | bytes 393220
  5.3 0.8 %copy-start.6 = (f32[2,64,128]{2,1,0:T(8,128)S(1)}, f32[2,64,128]{2,1,0:T(8,128)}, u32[]{:S(2)}) copy-start(f32[2,64,128]{2,1,0:T(8,128)} %constant.14.clone.phi_ref) | copy-start | bytes 196612
  6.1 0.8 %copy-start.7 = (bf16[128,192]{1,0:T(8,128)(2,1)S(1)}, bf16[128,192]{1,0:T(8,128)(2,1)}, u32[]{:S(2)}) copy-start(bf16[128,192]{1,0:T(8,128)(2,1)} %constant.13.clone.outer3_ref) | copy-start | bytes 147460
  7.0 0.8 %copy-start.8 = (bf16[2,64,128]{2,1,0:T(8,128)(2,1)S(1)}, bf16[2,64,128]{2,1,0:T(8,128)(2,1)}, u32[]{:S(2)}) copy-start(bf16[2,64,128]{2,1,0:T(8,128)(2,1)} %constant.17.clone.back_ref) | copy-start | bytes 98308
  7.7 0.8 %copy-start.9 = (bf16[128,128]{1,0:T(8,128)(2,1)S(1)}, bf16[128,128]{1,0:T(8,128)(2,1)}, u32[]{:S(2)}) copy-start(bf16[128,128]{1,0:T(8,128)(2,1)} %constant.12.clone.outer_ref) | copy-start | bytes 98308
  43.8 0.9 %copy-start.1 = (bf16[1,64,1024]{2,1,0:T(8,128)(2,1)S(1)}, bf16[1,64,1024]{2,1,0:T(8,128)(2,1)}, u32[]{:S(2)}) copy-start(bf16[1,64,1024]{2,1,0:T(8,128)(2,1)} %g_ref.1) | copy-start | bytes 393220
  43.8 0.9 %copy-start.10 = (f32[64]{0:T(128)S(1)}, f32[64]{0:T(128)}, u32[]{:S(2)}) copy-start(f32[64]{0:T(128)} %param.13) | copy-start | bytes 772

commit v2 on v1

--- a/solution.py
+++ b/solution.py
@@ -96,15 +96,29 @@
 
 def kernel(
     groups, parts, count, half,
+    x_hbm, g_hbm, f_hbm, outer_hbm, outer3_hbm, phi_hbm, inner_hbm, inner_t_hbm, back_hbm,
+    out_ref,
     x_ref, g_ref, f_ref, outer_ref, outer3_ref, phi_ref, inner_ref, inner_t_ref, back_ref,
-    out_ref,
     send_gx, send_f, recv_gx, recv_f, send_out,
-    gx_send, gx_recv, f_send, f_recv, out_send, out_recv,
+    load_sem, gx_send, gx_recv, f_send, f_recv, out_send, out_recv,
 ):
     devices = groups * parts
     rows = x_ref.shape[2] // LANES
     group, part = lax.axis_index("dp"), lax.axis_index("ctx")
     me = group * parts + part
+
+    loads = [
+        pltpu.make_async_copy(source, target, load_sem.at[n])
+        for n, (source, target) in enumerate(
+            [
+                (g_hbm, g_ref), (x_hbm, x_ref), (f_hbm, f_ref),
+                (outer_hbm, outer_ref), (outer3_hbm, outer3_ref), (phi_hbm, phi_ref),
+                (inner_hbm, inner_ref), (inner_t_hbm, inner_t_ref), (back_hbm, back_ref),
+            ]
+        )
+    ]
+    for load in loads:
+        load.start()
 
     barrier = pltpu.get_barrier_semaphore()
 
@@ -116,6 +130,8 @@
             device_id_type=MESH,
         )
 
+    for load in loads[:3]:
+        load.wait()
     for i in range(count):
         own = slice(i * devices, (i + 1) * devices)
         for r in range(rows):
@@ -177,6 +193,9 @@
     for i in range(count):
         recv_gx[i, group, part] = send_gx[i, me]
         recv_f[i, part] = send_f[i, me]
+
+    for load in loads[3:]:
+        load.wait()
 
     def product3(left, right):
         (left_high, left_low), (right_high, right_low) = left, right
@@ -268,18 +287,21 @@
         np.stack(np_split(inner.T)),
         np.stack(np_split(back)),
     )
+    tables = tuple(jnp.asarray(t) for t in tables)
+    operands = (inputs, cotangent, filters) + tables
     tile = (rows, LANES)
     out = pl.pallas_call(
         functools.partial(kernel, groups, parts, count, half),
         out_shape=jax.ShapeDtypeStruct((channels, 2) + tile, jnp.float32),
-        in_specs=[pl.BlockSpec(memory_space=pltpu.VMEM)] * 9,
+        in_specs=[pl.BlockSpec(memory_space=pltpu.HBM)] * 9,
         out_specs=pl.BlockSpec(memory_space=pltpu.VMEM),
-        scratch_shapes=[
+        scratch_shapes=[pltpu.VMEM(t.shape, t.dtype) for t in operands] + [
             pltpu.VMEM((count, devices, 2) + tile, jnp.float32),
             pltpu.VMEM((count, devices) + tile, jnp.float32),
             pltpu.VMEM((count, groups, parts, 2) + tile, jnp.float32),
             pltpu.VMEM((count, parts) + tile, jnp.float32),
             pltpu.VMEM((count, groups, parts, 2) + tile, jnp.float32),
+            pltpu.SemaphoreType.DMA((len(operands),)),
             pltpu.SemaphoreType.DMA((count, devices)),
             pltpu.SemaphoreType.DMA((count, devices)),
             pltpu.SemaphoreType.DMA((count, parts)),
@@ -290,7 +312,7 @@
         compiler_params=pltpu.CompilerParams(
             collective_id=0, has_side_effects=True, vmem_limit_bytes=40 * 2**20
         ),
-    )(inputs, cotangent, filters, *(jnp.asarray(t) for t in tables))
+    )(*operands)
     through = out[:, 0].reshape(channels, width)
     input_grad = through + skip_gain[:, None] * cotangent[0].astype(jnp.float32)
     return input_grad.astype(jnp.bfloat16)[None], out[:, 1].reshape(channels, width)

time: 46 us -> 47 us (1.022)
  Pallas kernels: 34.6 us -> 35.6 us
    pallas_call x1, Pallas kernels: 34.6 us -> 35.6 us  [fused_body(): pl.pallas_call(functools.partial(kernel, groups, parts, count, half), out...]
where the time goes in v2:
time: 47 us; the launch traced here: 46.5 us
  Pallas kernels  35.6 us (76%)
  local copies, waits for them, and re-layouts  9.53 us (20%)
  other arithmetic  0.75 us (2%)
  between operations  0.67 us (1%)
    pallas_call x1, Pallas kernels, fused_body(): pl.pallas_call(functools.partial(kernel, groups, parts, count, half), out...  35.6 us
    unnamed x23, local copies, waits for them, and re-layouts  9.45 us

profile of v2, /device:TPU:0, one launch (start us, length us, event | category | flops | bytes accessed | tf_op | source)
XLA Modules:
  0.0 46.5 jit_solution(10889309161882154970)
XLA Ops:
  0.6 0.0 copy-start
  0.6 0.9 %copy-done = bf16[1,64,1024]{2,1,0:T(8,128)(2,1)S(1)} copy-done((bf16[1,64,1024]{2,1,0:T(8,128)(2,1)S(1)}, bf16[1,64,1024]{2,1,0:T(8,128)(2,1)}, u32[]{:S(2)}) %copy-start) | copy-done | bytes 131096
  1.5 0.0 copy-start.2
  1.5 0.9 %copy-done.2 = f32[64,1024]{1,0:T(8,128)S(1)} copy-done((f32[64,1024]{1,0:T(8,128)S(1)}, f32[64,1024]{1,0:T(8,128)}, u32[]{:S(2)}) %copy-start.2) | copy-done | bytes 262168
  2.5 0.0 copy-start.3
  2.5 0.9 %copy-done.3 = bf16[2,256,256]{2,1,0:T(8,128)(2,1)S(1)} copy-done((bf16[2,256,256]{2,1,0:T(8,128)(2,1)S(1)}, bf16[2,256,256]{2,1,0:T(8,128)(2,1)}, u32[]{:S(2)}) %copy-start.3) | copy-done | bytes 262168
  3.4 0.0 copy-start.4
  3.4 0.9 %copy-done.4 = bf16[2,256,256]{2,1,0:T(8,128)(2,1)S(1)} copy-done((bf16[2,256,256]{2,1,0:T(8,128)(2,1)S(1)}, bf16[2,256,256]{2,1,0:T(8,128)(2,1)}, u32[]{:S(2)}) %copy-start.4) | copy-done | bytes 262168
  4.4 0.0 copy-start.5
  4.4 0.9 %copy-done.5 = bf16[1,64,1024]{2,1,0:T(8,128)(2,1)S(1)} copy-done((bf16[1,64,1024]{2,1,0:T(8,128)(2,1)S(1)}, bf16[1,64,1024]{2,1,0:T(8,128)(2,1)}, u32[]{:S(2)}) %copy-start.5) | copy-done | bytes 131096
  5.3 0.0 copy-start.6
  5.3 0.8 %copy-done.6 = f32[2,64,128]{2,1,0:T(8,128)S(1)} copy-done((f32[2,64,128]{2,1,0:T(8,128)S(1)}, f32[2,64,128]{2,1,0:T(8,128)}, u32[]{:S(2)}) %copy-start.6) | copy-done | bytes 65560
  6.1 0.0 copy-start.7
  6.1 0.8 %copy-done.7 = bf16[128,192]{1,0:T(8,128)(2,1)S(1)} copy-done((bf16[128,192]{1,0:T(8,128)(2,1)S(1)}, bf16[128,192]{1,0:T(8,128)(2,1)}, u32[]{:S(2)}) %copy-start.7) | copy-done | bytes 49176
  7.0 0.0 copy-start.8
  7.0 0.8 %copy-done.8 = bf16[2,64,128]{2,1,0:T(8,128)(2,1)S(1)} copy-done((bf16[2,64,128]{2,1,0:T(8,128)(2,1)S(1)}, bf16[2,64,128]{2,1,0:T(8,128)(2,1)}, u32[]{:S(2)}) %copy-start.8) | copy-done | bytes 32792
  7.7 0.0 copy-start.9
  7.7 0.8 %copy-done.9 = bf16[128,128]{1,0:T(8,128)(2,1)S(1)} copy-done((bf16[128,128]{1,0:T(8,128)(2,1)S(1)}, bf16[128,128]{1,0:T(8,128)(2,1)}, u32[]{:S(2)}) %copy-start.9) | copy-done | bytes 32792
  8.5 35.6 %shard_map.113 = f32[64,2,8,128]{3,2,1,0:T(8,128)S(1)} custom-call(bf16[1,64,1024]{2,1,0:T(8,128)(2,1)S(1)} %copy-done.5, bf16[1,64,1024]{2,1,0:T(8,128)(2,1)S(1)} %copy-done, f32[64,1024]{1,0:T(8,128)S(1)} %copy-done.2, bf16[128,128]{1,0:T(8,128)(2,1)S(1)} %copy-done.9, bf16[128,192]{1,0:T(8,128)(2,1)S(1)} %copy-done.7, f32[2,64,128]{2,1,0:T(8,128)S(1)} %copy-done.6, ...), custom_call_target="tpu_custom_call" | custom-call | tf_op jit(solution)/shard_map/pallas_call | solution.py:293
  44.1 0.8 %copy.14 = f32[8,8,8,128]{3,1,2,0:T(8,128)} copy(f32[8,8,8,128]{3,2,1,0:T(8,128)S(1)} %bitcast.7) | data formatting | bytes 524288
  44.9 0.0 copy-start.1
  44.9 0.0 copy-start.10
  44.9 0.9 %copy-done.1 = bf16[1,64,1024]{2,1,0:T(8,128)(2,1)S(1)} copy-done((bf16[1,64,1024]{2,1,0:T(8,128)(2,1)S(1)}, bf16[1,64,1024]{2,1,0:T(8,128)(2,1)}, u32[]{:S(2)}) %copy-start.1) | copy-done | bytes 131096
  45.8 0.0 copy-done.10
  45.8 0.8 %add_convert_fusion = bf16[1,64,1024]{2,1,0:T(8,128)(2,1)} fusion(f32[1,64,1024]{2,1,0:T(8,128)S(1)} %reshape_squeeze.6, bf16[1,64,1024]{2,1,0:T(8,128)(2,1)S(1)} %copy-done.1, f32[64]{0:T(128)S(1)} %copy-done.10), kind=kLoop, calls=%fused_computation.1 | loop fusion | flops 262144 | bytes 524544 | tf_op jit(solution)/shard_map/convert_element_type | solution.py:318
  (2 shorter events, 0.1 us)
Async XLA Ops:
  0.6 0.9 %copy-start = (bf16[1,64,1024]{2,1,0:T(8,128)(2,1)S(1)}, bf16[1,64,1024]{2,1,0:T(8,128)(2,1)}, u32[]{:S(2)}) copy-start(bf16[1,64,1024]{2,1,0:T(8,128)(2,1)} %g_hbm.1) | copy-start | bytes 393220
  1.5 0.9 %copy-start.2 = (f32[64,1024]{1,0:T(8,128)S(1)}, f32[64,1024]{1,0:T(8,128)}, u32[]{:S(2)}) copy-start(f32[64,1024]{1,0:T(8,128)} %f_hbm.1) | copy-start | bytes 786436
  2.5 0.9 %copy-start.3 = (bf16[2,256,256]{2,1,0:T(8,128)(2,1)S(1)}, bf16[2,256,256]{2,1,0:T(8,128)(2,1)}, u32[]{:S(2)}) copy-start(bf16[2,256,256]{2,1,0:T(8,128)(2,1)} %constant.16.clone.inner_t_hbm) | copy-start | bytes 786436
  3.4 0.9 %copy-start.4 = (bf16[2,256,256]{2,1,0:T(8,128)(2,1)S(1)}, bf16[2,256,256]{2,1,0:T(8,128)(2,1)}, u32[]{:S(2)}) copy-start(bf16[2,256,256]{2,1,0:T(8,128)(2,1)} %constant.15.clone.inner_hbm) | copy-start | bytes 786436
  4.4 0.9 %copy-start.5 = (bf16[1,64,1024]{2,1,0:T(8,128)(2,1)S(1)}, bf16[1,64,1024]{2,1,0:T(8,128)(2,1)}, u32[]{:S(2)}) copy-start(bf16[1,64,1024]{2,1,0:T(8,128)(2,1)} %x_hbm.1) | copy-start | bytes 393220
  5.3 0.8 %copy-start.6 = (f32[2,64,128]{2,1,0:T(8,128)S(1)}, f32[2,64,128]{2,1,0:T(8,128)}, u32[]{:S(2)}) copy-start(f32[2,64,128]{2,1,0:T(8,128)} %constant.14.clone.phi_hbm) | copy-start | bytes 196612
  6.1 0.8 %copy-start.7 = (bf16[128,192]{1,0:T(8,128)(2,1)S(1)}, bf16[128,192]{1,0:T(8,128)(2,1)}, u32[]{:S(2)}) copy-start(bf16[128,192]{1,0:T(8,128)(2,1)} %constant.13.clone.outer3_hbm) | copy-start | bytes 147460
  7.0 0.8 %copy-start.8 = (bf16[2,64,128]{2,1,0:T(8,128)(2,1)S(1)}, bf16[2,64,128]{2,1,0:T(8,128)(2,1)}, u32[]{:S(2)}) copy-start(bf16[2,64,128]{2,1,0:T(8,128)(2,1)} %constant.17.clone.back_hbm) | copy-start | bytes 98308
  7.7 0.8 %copy-start.9 = (bf16[128,128]{1,0:T(8,128)(2,1)S(1)}, bf16[128,128]{1,0:T(8,128)(2,1)}, u32[]{:S(2)}) copy-start(bf16[128,128]{1,0:T(8,128)(2,1)} %constant.12.clone.outer_hbm) | copy-start | bytes 98308
  44.9 0.9 %copy-start.1 = (bf16[1,64,1024]{2,1,0:T(8,128)(2,1)S(1)}, bf16[1,64,1024]{2,1,0:T(8,128)(2,1)}, u32[]{:S(2)}) copy-start(bf16[1,64,1024]{2,1,0:T(8,128)(2,1)} %g_hbm.1) | copy-start | bytes 393220
  44.9 0.9 %copy-start.10 = (f32[64]{0:T(128)S(1)}, f32[64]{0:T(128)}, u32[]{:S(2)}) copy-start(f32[64]{0:T(128)} %param.13) | copy-start | bytes 772

commit v3 on v2

--- a/solution.py
+++ b/solution.py
@@ -97,10 +97,10 @@
 def kernel(
     groups, parts, count, half,
     x_hbm, g_hbm, f_hbm, outer_hbm, outer3_hbm, phi_hbm, inner_hbm, inner_t_hbm, back_hbm,
-    out_ref,
+    through_ref, filter_grad_ref,
     x_ref, g_ref, f_ref, outer_ref, outer3_ref, phi_ref, inner_ref, inner_t_ref, back_ref,
-    send_gx, send_f, recv_gx, recv_f, send_out,
-    load_sem, gx_send, gx_recv, f_send, f_recv, out_send, out_recv,
+    send_gx, send_f, recv_gx, recv_f, send_through, send_filter_grad,
+    load_sem, gx_sem, f_sem, through_sem, filter_grad_sem, relay_sem,
 ):
     devices = groups * parts
     rows = x_ref.shape[2] // LANES
@@ -120,19 +120,39 @@
     for load in loads:
         load.start()
 
+    def after(position, step, size):
+        moved = position + step
+        return jnp.where(moved >= size, moved - size, moved)
+
+    def each_other(act):
+        for lead in range(groups):
+            there = after(group, lead, groups)
+
+            @pl.loop(0 if lead else 1, parts)
+            def _(step):
+                act(there, after(part, step, parts))
+
     barrier = pltpu.get_barrier_semaphore()
-
-    @pl.loop(1, devices)
-    def _(step):
-        other = lax.rem(me + step, devices)
-        pl.semaphore_signal(
-            barrier, inc=1, device_id=(other // parts, lax.rem(other, parts)),
+    each_other(
+        lambda to_group, to_part: pl.semaphore_signal(
+            barrier, inc=1, device_id=(to_group, to_part), device_id_type=MESH
+        )
+    )
+
+    def remote(source, target, sems, i, to_group, to_part):
+        pltpu.make_async_remote_copy(
+            src_ref=source,
+            dst_ref=target,
+            send_sem=sems.at[0, i],
+            recv_sem=sems.at[1, i],
+            device_id=(to_group, to_part),
             device_id_type=MESH,
-        )
-
-    for load in loads[:3]:
-        load.wait()
-    for i in range(count):
+        ).start()
+
+    def wait_bytes(held, sem):
+        pltpu.make_async_copy(held, held, sem).wait()
+
+    def pack(i):
         own = slice(i * devices, (i + 1) * devices)
         for r in range(rows):
             lanes = slice(r * LANES, (r + 1) * LANES)
@@ -140,60 +160,31 @@
             send_gx[i, :, 1, r, :] = x_ref[0, own, lanes].astype(jnp.float32)
             send_f[i, :, r, :] = f_ref[own, lanes]
 
+    def send_rows(i):
+        @pl.loop(1, parts)
+        def _(step):
+            other = after(part, step, parts)
+            remote(
+                send_f.at[i, group * parts + other], recv_f.at[i, part], f_sem, i, group, other
+            )
+
+        each_other(
+            lambda to_group, to_part: remote(
+                send_gx.at[i, to_group * parts + to_part], recv_gx.at[i, me],
+                gx_sem, i, to_group, to_part,
+            )
+        )
+        recv_gx[i, me] = send_gx[i, me]
+        recv_f[i, part] = send_f[i, me]
+
+    for load in loads[:3]:
+        load.wait()
+    pack(0)
     pl.semaphore_wait(barrier, devices - 1)
-
-    def filter_copy(i, step, to):
-        other = lax.rem(part + step, parts) if to else lax.rem(part - step + parts, parts)
-        return pltpu.make_async_remote_copy(
-            src_ref=send_f.at[i, group * parts + other],
-            dst_ref=recv_f.at[i, part if to else other],
-            send_sem=f_send.at[i, step],
-            recv_sem=f_recv.at[i, step],
-            device_id=(group, other),
-            device_id_type=MESH,
-        )
-
-    def row_copy(i, step, to):
-        lead, rest = step // parts, lax.rem(step, parts)
-        if to:
-            there = (lax.rem(group + lead, groups), lax.rem(part + rest, parts))
-            slot = (group, part)
-        else:
-            there = (lax.rem(group - lead + groups, groups), lax.rem(part - rest + parts, parts))
-            slot = there
-        return pltpu.make_async_remote_copy(
-            src_ref=send_gx.at[i, there[0] * parts + there[1]],
-            dst_ref=recv_gx.at[i, slot[0], slot[1]],
-            send_sem=gx_send.at[i, step],
-            recv_sem=gx_recv.at[i, step],
-            device_id=there,
-            device_id_type=MESH,
-        )
-
-    def out_copy(i, step, to):
-        lead, rest = step // parts, lax.rem(step, parts)
-        if to:
-            there = (lax.rem(group + lead, groups), lax.rem(part + rest, parts))
-            channel = i * devices + me
-        else:
-            there = (lax.rem(group - lead + groups, groups), lax.rem(part - rest + parts, parts))
-            channel = i * devices + there[0] * parts + there[1]
-        return pltpu.make_async_remote_copy(
-            src_ref=send_out.at[i, there[0], there[1]],
-            dst_ref=out_ref.at[channel],
-            send_sem=out_send.at[i, step],
-            recv_sem=out_recv.at[i, step],
-            device_id=there,
-            device_id_type=MESH,
-        )
-
-    for i in range(count):
-        pl.loop(1, parts)(lambda step: filter_copy(i, step, True).start())
-        pl.loop(1, devices)(lambda step: row_copy(i, step, True).start())
-    for i in range(count):
-        recv_gx[i, group, part] = send_gx[i, me]
-        recv_f[i, part] = send_f[i, me]
-
+    send_rows(0)
+    for i in range(1, count):
+        pack(i)
+        send_rows(i)
     for load in loads[3:]:
         load.wait()
 
@@ -208,11 +199,11 @@
         return real * cosine - imag * sine, real * sine + imag * cosine
 
     for i in range(count):
-        pl.loop(1, parts)(lambda step: filter_copy(i, step, False).wait_recv())
-        pl.loop(1, devices)(lambda step: row_copy(i, step, False).wait_recv())
+        wait_bytes(recv_f.at[i, pl.ds(0, parts - 1)], f_sem.at[1, i])
+        wait_bytes(recv_gx.at[i, pl.ds(0, devices - 1)], gx_sem.at[1, i])
 
         def signal(kind, b):
-            return recv_gx[i, b, :, kind].reshape(half, LANES).astype(jnp.bfloat16)
+            return recv_gx[i, b * parts:(b + 1) * parts, kind].reshape(half, LANES).astype(jnp.bfloat16)
 
         exact = jnp.concatenate(
             [signal(0, b) for b in range(groups)] + [signal(1, b) for b in range(groups)], axis=1
@@ -257,19 +248,50 @@
             pair = turn(block[:, :LANES], block[:, LANES:], -phi_ref[1])
             turned.append(jnp.concatenate(pair, axis=0))
         final = product3((back_ref[0], back_ref[1]), split(jnp.concatenate(turned, axis=1)))
-        filter_grad = final[:, groups * LANES:].reshape(parts, rows, LANES)
+        send_filter_grad[i] = final[:, groups * LANES:].reshape(parts, rows, LANES)
         for b in range(groups):
             through = final[:, b * LANES:(b + 1) * LANES]
-            send_out[i, b, :, 0] = through.reshape(parts, rows, LANES)
-            send_out[i, b, :, 1] = filter_grad
-        pl.loop(1, devices)(lambda step: out_copy(i, step, True).start())
-        out_ref[i * devices + me] = send_out[i, group, part]
+            send_through[i, b * parts:(b + 1) * parts] = through.reshape(parts, rows, LANES)
+
+        channel = i * devices + me
+
+        @pl.loop(1, parts)
+        def _(step):
+            other = after(part, step, parts)
+            remote(
+                send_filter_grad.at[i, other], filter_grad_ref.at[channel],
+                filter_grad_sem, i, group, other,
+            )
+
+        each_other(
+            lambda to_group, to_part: remote(
+                send_through.at[i, to_group * parts + to_part], through_ref.at[channel],
+                through_sem, i, to_group, to_part,
+            )
+        )
+        filter_grad_ref[channel] = send_filter_grad[i, part]
+        through_ref[channel] = send_through[i, me]
+
+    def held_by(i, b):
+        return filter_grad_ref.at[pl.ds(i * devices + b * parts, parts)]
 
     for i in range(count):
-        pl.loop(1, parts)(lambda step: filter_copy(i, step, True).wait_send())
-        pl.loop(1, devices)(lambda step: row_copy(i, step, True).wait_send())
-        pl.loop(1, devices)(lambda step: out_copy(i, step, True).wait_send())
-        pl.loop(1, devices)(lambda step: out_copy(i, step, False).wait_recv())
+        wait_bytes(
+            filter_grad_ref.at[pl.ds(i * devices, parts - 1)], filter_grad_sem.at[1, i]
+        )
+        for lead in range(1, groups):
+            remote(
+                held_by(i, group), held_by(i, group), relay_sem, i, after(group, lead, groups), part
+            )
+
+    for i in range(count):
+        wait_bytes(send_f.at[i, pl.ds(0, parts - 1)], f_sem.at[0, i])
+        wait_bytes(send_gx.at[i, pl.ds(0, devices - 1)], gx_sem.at[0, i])
+        wait_bytes(send_filter_grad.at[i, pl.ds(0, parts - 1)], filter_grad_sem.at[0, i])
+        for side in range(2):
+            wait_bytes(send_through.at[i, pl.ds(0, devices - 1)], through_sem.at[side, i])
+            relayed = pl.ds(i * devices, (groups - 1) * parts)
+            wait_bytes(filter_grad_ref.at[relayed], relay_sem.at[side, i])
 
 
 def fused_body(groups, parts, inputs, cotangent, filters, skip_gain):
@@ -290,32 +312,26 @@
     tables = tuple(jnp.asarray(t) for t in tables)
     operands = (inputs, cotangent, filters) + tables
     tile = (rows, LANES)
-    out = pl.pallas_call(
+    whole = jax.ShapeDtypeStruct((channels,) + tile, jnp.float32)
+    through, filter_grad = pl.pallas_call(
         functools.partial(kernel, groups, parts, count, half),
-        out_shape=jax.ShapeDtypeStruct((channels, 2) + tile, jnp.float32),
-        in_specs=[pl.BlockSpec(memory_space=pltpu.HBM)] * 9,
-        out_specs=pl.BlockSpec(memory_space=pltpu.VMEM),
+        out_shape=(whole, whole),
+        in_specs=[pl.BlockSpec(memory_space=pltpu.HBM)] * len(operands),
+        out_specs=(pl.BlockSpec(memory_space=pltpu.VMEM),) * 2,
         scratch_shapes=[pltpu.VMEM(t.shape, t.dtype) for t in operands] + [
             pltpu.VMEM((count, devices, 2) + tile, jnp.float32),
             pltpu.VMEM((count, devices) + tile, jnp.float32),
-            pltpu.VMEM((count, groups, parts, 2) + tile, jnp.float32),
+            pltpu.VMEM((count, devices, 2) + tile, jnp.float32),
             pltpu.VMEM((count, parts) + tile, jnp.float32),
-            pltpu.VMEM((count, groups, parts, 2) + tile, jnp.float32),
+            pltpu.VMEM((count, devices) + tile, jnp.float32),
+            pltpu.VMEM((count, parts) + tile, jnp.float32),
             pltpu.SemaphoreType.DMA((len(operands),)),
-            pltpu.SemaphoreType.DMA((count, devices)),
-            pltpu.SemaphoreType.DMA((count, devices)),
-            pltpu.SemaphoreType.DMA((count, parts)),
-            pltpu.SemaphoreType.DMA((count, parts)),
-            pltpu.SemaphoreType.DMA((count, devices)),
-            pltpu.SemaphoreType.DMA((count, devices)),
-        ],
-        compiler_params=pltpu.CompilerParams(
-            collective_id=0, has_side_effects=True, vmem_limit_bytes=40 * 2**20
-        ),
+        ] + [pltpu.SemaphoreType.DMA((2, count))] * 5,
+        compiler_params=pltpu.CompilerParams(collective_id=0, has_side_effects=True),
     )(*operands)
-    through = out[:, 0].reshape(channels, width)
+    through = through.reshape(channels, width)
     input_grad = through + skip_gain[:, None] * cotangent[0].astype(jnp.float32)
-    return input_grad.astype(jnp.bfloat16)[None], out[:, 1].reshape(channels, width)
+    return input_grad.astype(jnp.bfloat16)[None], filter_grad.reshape(channels, width)
 
 
 def solution(mesh):

time: 47 us -> 35.8 us (0.76)
  local copies, waits for them, and re-layouts: 9.53 us -> 1.98 us
  Pallas kernels: 35.6 us -> 32.1 us
    unnamed x23 -> x7, local copies, waits for them, and re-layouts: 9.45 us -> 0.95 us
    pallas_call x1, Pallas kernels: 35.6 us -> 32.1 us  [fused_body(): pl.pallas_call(functools.partial(kernel, groups, parts, count, half), out...]
    reshape x0 -> x1, local copies, waits for them, and re-layouts: none -> 1.03 us  [fused_body(): through = through.reshape(channels, width)]
where the time goes in v3:
time: 35.8 us; the launch traced here: 35.6 us
  Pallas kernels  32.1 us (90%)
  local copies, waits for them, and re-layouts  1.98 us (6%)
  other arithmetic  0.75 us (2%)
  between operations  0.68 us (2%)
    pallas_call x1, Pallas kernels, fused_body(): pl.pallas_call(functools.partial(kernel, groups, parts, count, half), out...  32.1 us
    reshape x1, local copies, waits for them, and re-layouts, fused_body(): through = through.reshape(channels, width)  1.03 us
    unnamed x7, local copies, waits for them, and re-layouts  0.95 us
    convert_element_type x1, other arithmetic, fused_body(): input_grad.astype(jnp.bfloat16)[None]  0.75 us

profile of v3, /device:TPU:0, one launch (start us, length us, event | category | flops | bytes accessed | tf_op | source)
XLA Modules:
  0.0 35.6 jit_solution(9463205226310490156)
XLA Ops:
  0.6 32.1 %shard_map.113 = (f32[64,8,128]{2,1,0:T(8,128)}, f32[64,8,128]{2,1,0:T(8,128)}) custom-call(bf16[1,64,1024]{2,1,0:T(8,128)(2,1)} %x_hbm.1, bf16[1,64,1024]{2,1,0:T(8,128)(2,1)} %g_hbm.1, f32[64,1024]{1,0:T(8,128)} %f_hbm.1, bf16[128,128]{1,0:T(8,128)(2,1)} %constant.12.clone.outer_hbm, bf16[128,192]{1,0:T(8,128)(2,1)} %constant.13.clone.outer3_hbm, ...), custom_call_target="tpu_custom_call" | custom-call | tf_op jit(solution)/shard_map/pallas_call | solution.py:316
  32.8 0.0 copy-start
  32.8 0.0 copy-start.2
  32.8 1.0 %reshape.17 = f32[1,64,1024]{2,1,0:T(8,128)S(1)} reshape(f32[64,8,128]{2,1,0:T(8,128)} %get-tuple-element.4) | data formatting | bytes 524288 | tf_op jit(solution)/shard_map/reshape | solution.py:332
  33.8 0.0 copy-done
  33.9 0.0 copy-done.2
  33.9 0.0 copy-start.1
  33.9 0.8 %add_convert_fusion = bf16[1,64,1024]{2,1,0:T(8,128)(2,1)} fusion(f32[1,64,1024]{2,1,0:T(8,128)S(1)} %reshape.17, bf16[1,64,1024]{2,1,0:T(8,128)(2,1)S(1)} %copy-done, f32[64]{0:T(128)S(1)} %copy-done.2), kind=kLoop, calls=%fused_computation.1 | loop fusion | flops 262144 | bytes 524544 | tf_op jit(solution)/shard_map/convert_element_type | solution.py:334
  34.6 0.2 copy-done.1
  34.8 0.8 %copy.14 = f32[8,8,8,128]{3,1,2,0:T(8,128)} copy(f32[8,8,8,128]{3,2,1,0:T(8,128)S(1)} %bitcast.4) | data formatting | bytes 524288
Async XLA Ops:
  32.8 1.1 %copy-start = (bf16[1,64,1024]{2,1,0:T(8,128)(2,1)S(1)}, bf16[1,64,1024]{2,1,0:T(8,128)(2,1)}, u32[]{:S(2)}) copy-start(bf16[1,64,1024]{2,1,0:T(8,128)(2,1)} %g_hbm.1) | copy-start | bytes 393220
  32.8 1.1 %copy-start.2 = (f32[64]{0:T(128)S(1)}, f32[64]{0:T(128)}, u32[]{:S(2)}) copy-start(f32[64]{0:T(128)} %param.13) | copy-start | bytes 772
  33.9 1.0 %copy-start.1 = (f32[64,8,128]{2,1,0:T(8,128)S(1)}, f32[64,8,128]{2,1,0:T(8,128)}, u32[]{:S(2)}) copy-start(f32[64,8,128]{2,1,0:T(8,128)} %get-tuple-element.5) | copy-start | bytes 786436

commit v4 on v3

--- a/solution.py
+++ b/solution.py
@@ -139,12 +139,12 @@
         )
     )
 
-    def remote(source, target, sems, i, to_group, to_part):
+    def remote(source, target, send_sem, recv_sem, to_group, to_part):
         pltpu.make_async_remote_copy(
             src_ref=source,
             dst_ref=target,
-            send_sem=sems.at[0, i],
-            recv_sem=sems.at[1, i],
+            send_sem=send_sem,
+            recv_sem=recv_sem,
             device_id=(to_group, to_part),
             device_id_type=MESH,
         ).start()
@@ -156,35 +156,32 @@
         own = slice(i * devices, (i + 1) * devices)
         for r in range(rows):
             lanes = slice(r * LANES, (r + 1) * LANES)
-            send_gx[i, :, 0, r, :] = g_ref[0, own, lanes].astype(jnp.float32)
-            send_gx[i, :, 1, r, :] = x_ref[0, own, lanes].astype(jnp.float32)
-            send_f[i, :, r, :] = f_ref[own, lanes]
-
-    def send_rows(i):
-        @pl.loop(1, parts)
-        def _(step):
-            other = after(part, step, parts)
-            remote(
-                send_f.at[i, group * parts + other], recv_f.at[i, part], f_sem, i, group, other
-            )
-
-        each_other(
-            lambda to_group, to_part: remote(
-                send_gx.at[i, to_group * parts + to_part], recv_gx.at[i, me],
-                gx_sem, i, to_group, to_part,
-            )
-        )
-        recv_gx[i, me] = send_gx[i, me]
-        recv_f[i, part] = send_f[i, me]
+            send_gx[:, i, 0, r, :] = g_ref[0, own, lanes].astype(jnp.float32)
+            send_gx[:, i, 1, r, :] = x_ref[0, own, lanes].astype(jnp.float32)
+            send_f[:, i, r, :] = f_ref[own, lanes]
 
     for load in loads[:3]:
         load.wait()
-    pack(0)
+    for i in range(count):
+        pack(i)
     pl.semaphore_wait(barrier, devices - 1)
-    send_rows(0)
-    for i in range(1, count):
-        pack(i)
-        send_rows(i)
+
+    @pl.loop(1, parts)
+    def _(step):
+        other = after(part, step, parts)
+        remote(
+            send_f.at[group * parts + other], recv_f.at[part],
+            f_sem.at[0], f_sem.at[1], group, other,
+        )
+
+    each_other(
+        lambda to_group, to_part: remote(
+            send_gx.at[to_group * parts + to_part], recv_gx.at[me],
+            gx_sem.at[0], gx_sem.at[1], to_group, to_part,
+        )
+    )
+    recv_gx[me] = send_gx[me]
+    recv_f[part] = send_f[me]
     for load in loads[3:]:
         load.wait()
 
@@ -198,17 +195,18 @@
         cosine = phi_ref[0]
         return real * cosine - imag * sine, real * sine + imag * cosine
 
+    wait_bytes(recv_f.at[pl.ds(0, parts - 1)], f_sem.at[1])
+    wait_bytes(recv_gx.at[pl.ds(0, devices - 1)], gx_sem.at[1])
+
     for i in range(count):
-        wait_bytes(recv_f.at[i, pl.ds(0, parts - 1)], f_sem.at[1, i])
-        wait_bytes(recv_gx.at[i, pl.ds(0, devices - 1)], gx_sem.at[1, i])
 
         def signal(kind, b):
-            return recv_gx[i, b * parts:(b + 1) * parts, kind].reshape(half, LANES).astype(jnp.bfloat16)
+            return recv_gx[b * parts:(b + 1) * parts, i, kind].reshape(half, LANES).astype(jnp.bfloat16)
 
         exact = jnp.concatenate(
             [signal(0, b) for b in range(groups)] + [signal(1, b) for b in range(groups)], axis=1
         )
-        high, low = split(recv_f[i].reshape(half, LANES))
+        high, low = split(recv_f[:, i].reshape(half, LANES))
         stepped = dot(outer_ref[...], jnp.concatenate([exact, exact], axis=0))
         filter_part = dot(outer3_ref[...], jnp.concatenate([high, high, low], axis=0))
         stepped = jnp.concatenate([stepped, filter_part], axis=1)
@@ -260,13 +258,13 @@
             other = after(part, step, parts)
             remote(
                 send_filter_grad.at[i, other], filter_grad_ref.at[channel],
-                filter_grad_sem, i, group, other,
+                filter_grad_sem.at[0, i], filter_grad_sem.at[1, i], group, other,
             )
 
         each_other(
             lambda to_group, to_part: remote(
                 send_through.at[i, to_group * parts + to_part], through_ref.at[channel],
-                through_sem, i, to_group, to_part,
+                through_sem.at[0, i], through_sem.at[1, i], to_group, to_part,
             )
         )
         filter_grad_ref[channel] = send_filter_grad[i, part]
@@ -281,12 +279,13 @@
         )
         for lead in range(1, groups):
             remote(
-                held_by(i, group), held_by(i, group), relay_sem, i, after(group, lead, groups), part
+                held_by(i, group), held_by(i, group), relay_sem.at[0, i], relay_sem.at[1, i],
+                after(group, lead, groups), part,
             )
 
+    wait_bytes(send_f.at[pl.ds(0, parts - 1)], f_sem.at[0])
+    wait_bytes(send_gx.at[pl.ds(0, devices - 1)], gx_sem.at[0])
     for i in range(count):
-        wait_bytes(send_f.at[i, pl.ds(0, parts - 1)], f_sem.at[0, i])
-        wait_bytes(send_gx.at[i, pl.ds(0, devices - 1)], gx_sem.at[0, i])
         wait_bytes(send_filter_grad.at[i, pl.ds(0, parts - 1)], filter_grad_sem.at[0, i])
         for side in range(2):
             wait_bytes(send_through.at[i, pl.ds(0, devices - 1)], through_sem.at[side, i])
@@ -319,14 +318,14 @@
         in_specs=[pl.BlockSpec(memory_space=pltpu.HBM)] * len(operands),
         out_specs=(pl.BlockSpec(memory_space=pltpu.VMEM),) * 2,
         scratch_shapes=[pltpu.VMEM(t.shape, t.dtype) for t in operands] + [
-            pltpu.VMEM((count, devices, 2) + tile, jnp.float32),
-            pltpu.VMEM((count, devices) + tile, jnp.float32),
-            pltpu.VMEM((count, devices, 2) + tile, jnp.float32),
-            pltpu.VMEM((count, parts) + tile, jnp.float32),
+            pltpu.VMEM((devices, count, 2) + tile, jnp.float32),
+            pltpu.VMEM((devices, count) + tile, jnp.float32),
+            pltpu.VMEM((devices, count, 2) + tile, jnp.float32),
+            pltpu.VMEM((parts, count) + tile, jnp.float32),
             pltpu.VMEM((count, devices) + tile, jnp.float32),
             pltpu.VMEM((count, parts) + tile, jnp.float32),
             pltpu.SemaphoreType.DMA((len(operands),)),
-        ] + [pltpu.SemaphoreType.DMA((2, count))] * 5,
+        ] + [pltpu.SemaphoreType.DMA((2,))] * 2 + [pltpu.SemaphoreType.DMA((2, count))] * 3,
         compiler_params=pltpu.CompilerParams(collective_id=0, has_side_effects=True),
     )(*operands)
     through = through.reshape(channels, width)

time: 35.8 us -> 38.4 us (1.073)
  Pallas kernels: 32.1 us -> 34.8 us
    pallas_call x1, Pallas kernels: 32.1 us -> 34.8 us  [fused_body(): pl.pallas_call(functools.partial(kernel, groups, parts, count, half), out...]
where the time goes in v4:
time: 38.4 us; the launch traced here: 38.2 us
  Pallas kernels  34.8 us (91%)
  local copies, waits for them, and re-layouts  1.98 us (5%)
  other arithmetic  0.75 us (2%)
  between operations  0.68 us (2%)
    pallas_call x1, Pallas kernels, fused_body(): pl.pallas_call(functools.partial(kernel, groups, parts, count, half), out...  34.8 us
    reshape x1, local copies, waits for them, and re-layouts, fused_body(): through = through.reshape(channels, width)  1.03 us
    unnamed x7, local copies, waits for them, and re-layouts  0.95 us

profile of v4, /device:TPU:0, one launch (start us, length us, event | category | flops | bytes accessed | tf_op | source)
XLA Modules:
  0.0 38.2 jit_solution(14655445388833315932)
XLA Ops:
  0.6 34.8 %shard_map.113 = (f32[64,8,128]{2,1,0:T(8,128)}, f32[64,8,128]{2,1,0:T(8,128)}) custom-call(bf16[1,64,1024]{2,1,0:T(8,128)(2,1)} %x_hbm.1, bf16[1,64,1024]{2,1,0:T(8,128)(2,1)} %g_hbm.1, f32[64,1024]{1,0:T(8,128)} %f_hbm.1, bf16[128,128]{1,0:T(8,128)(2,1)} %constant.12.clone.outer_hbm, bf16[128,192]{1,0:T(8,128)(2,1)} %constant.13.clone.outer3_hbm, ...), custom_call_target="tpu_custom_call" | custom-call | tf_op jit(solution)/shard_map/pallas_call | solution.py:315
  35.4 0.0 copy-start
  35.5 0.0 copy-start.2
  35.5 1.0 %reshape.17 = f32[1,64,1024]{2,1,0:T(8,128)S(1)} reshape(f32[64,8,128]{2,1,0:T(8,128)} %get-tuple-element.4) | data formatting | bytes 524288 | tf_op jit(solution)/shard_map/reshape | solution.py:331
  36.5 0.0 copy-done
  36.5 0.0 copy-done.2
  36.5 0.0 copy-start.1
  36.5 0.8 %add_convert_fusion = bf16[1,64,1024]{2,1,0:T(8,128)(2,1)} fusion(f32[1,64,1024]{2,1,0:T(8,128)S(1)} %reshape.17, bf16[1,64,1024]{2,1,0:T(8,128)(2,1)S(1)} %copy-done, f32[64]{0:T(128)S(1)} %copy-done.2), kind=kLoop, calls=%fused_computation.1 | loop fusion | flops 262144 | bytes 524544 | tf_op jit(solution)/shard_map/convert_element_type | solution.py:333
  37.3 0.2 copy-done.1
  37.5 0.8 %copy.14 = f32[8,8,8,128]{3,1,2,0:T(8,128)} copy(f32[8,8,8,128]{3,2,1,0:T(8,128)S(1)} %bitcast.4) | data formatting | bytes 524288
Async XLA Ops:
  35.4 1.1 %copy-start = (bf16[1,64,1024]{2,1,0:T(8,128)(2,1)S(1)}, bf16[1,64,1024]{2,1,0:T(8,128)(2,1)}, u32[]{:S(2)}) copy-start(bf16[1,64,1024]{2,1,0:T(8,128)(2,1)} %g_hbm.1) | copy-start | bytes 393220
  35.5 1.1 %copy-start.2 = (f32[64]{0:T(128)S(1)}, f32[64]{0:T(128)}, u32[]{:S(2)}) copy-start(f32[64]{0:T(128)} %param.13) | copy-start | bytes 772
  36.5 1.0 %copy-start.1 = (f32[64,8,128]{2,1,0:T(8,128)S(1)}, f32[64,8,128]{2,1,0:T(8,128)}, u32[]{:S(2)}) copy-start(f32[64,8,128]{2,1,0:T(8,128)} %get-tuple-element.5) | copy-start | bytes 786436

commit v5 on v3

--- a/solution.py
+++ b/solution.py
@@ -152,15 +152,11 @@
     def wait_bytes(held, sem):
         pltpu.make_async_copy(held, held, sem).wait()
 
-    def pack(i):
-        own = slice(i * devices, (i + 1) * devices)
+    def pack(target, source):
         for r in range(rows):
-            lanes = slice(r * LANES, (r + 1) * LANES)
-            send_gx[i, :, 0, r, :] = g_ref[0, own, lanes].astype(jnp.float32)
-            send_gx[i, :, 1, r, :] = x_ref[0, own, lanes].astype(jnp.float32)
-            send_f[i, :, r, :] = f_ref[own, lanes]
-
-    def send_rows(i):
+            target[:, r, :] = source[:, r * LANES:(r + 1) * LANES].astype(jnp.float32)
+
+    def send_filters(i):
         @pl.loop(1, parts)
         def _(step):
             other = after(part, step, parts)
@@ -168,92 +164,116 @@
                 send_f.at[i, group * parts + other], recv_f.at[i, part], f_sem, i, group, other
             )
 
+        recv_f[i, part] = send_f[i, me]
+
+    def send_rows(i, kind):
         each_other(
             lambda to_group, to_part: remote(
-                send_gx.at[i, to_group * parts + to_part], recv_gx.at[i, me],
-                gx_sem, i, to_group, to_part,
-            )
-        )
-        recv_gx[i, me] = send_gx[i, me]
-        recv_f[i, part] = send_f[i, me]
-
-    for load in loads[:3]:
-        load.wait()
-    pack(0)
-    pl.semaphore_wait(barrier, devices - 1)
-    send_rows(0)
-    for i in range(1, count):
-        pack(i)
-        send_rows(i)
+                send_gx.at[i, kind, to_group * parts + to_part], recv_gx.at[i, kind, me],
+                gx_sem, 2 * i + kind, to_group, to_part,
+            )
+        )
+        recv_gx[i, kind, me] = send_gx[i, kind, me]
+
+    for i in range(count):
+        own = slice(i * devices, (i + 1) * devices)
+        for kind, source in enumerate((g_ref, x_ref)):
+            if i == 0:
+                loads[kind].wait()
+            if kind == 0:
+                if i == 0:
+                    loads[2].wait()
+                pack(send_f.at[i], f_ref.at[own])
+            pack(send_gx.at[i, kind], source.at[0, own])
+            if i == 0 and kind == 0:
+                pl.semaphore_wait(barrier, devices - 1)
+            if kind == 0:
+                send_filters(i)
+            send_rows(i, kind)
     for load in loads[3:]:
         load.wait()
-
-    def product3(left, right):
-        (left_high, left_low), (right_high, right_low) = left, right
-        return (
-            dot(left_high, right_high) + dot(left_low, right_high) + dot(left_high, right_low)
-        )
 
     def turn(real, imag, sine):
         cosine = phi_ref[0]
         return real * cosine - imag * sine, real * sine + imag * cosine
 
+    def along_lanes(pairs, table_ref):
+        values = jnp.concatenate([jnp.concatenate(pair, axis=1) for pair in pairs], axis=0)
+        high, low = split(values)
+        out = dot(jnp.concatenate([high, low, high], axis=1), table_ref[...])
+        blocks = [out[s * half:(s + 1) * half] for s in range(len(pairs))]
+        return [(block[:, :LANES], block[:, LANES:]) for block in blocks]
+
+    def forward(stepped):
+        blocks = [stepped[:, s:s + LANES] for s in range(0, stepped.shape[1], LANES)]
+        pairs = [turn(block[:half], block[half:], phi_ref[1]) for block in blocks]
+        return along_lanes(pairs, inner_ref)
+
+    def backward(specs):
+        pairs = [turn(real, imag, -phi_ref[1]) for real, imag in along_lanes(specs, inner_t_ref)]
+        values = jnp.concatenate([jnp.concatenate(pair, axis=0) for pair in pairs], axis=1)
+        high, low = split(values)
+        out = dot(back_ref[...], jnp.concatenate([high, high, low], axis=0))
+        return [
+            out[:, s:s + LANES].reshape(parts, rows, LANES) for s in range(0, out.shape[1], LANES)
+        ]
+
+    def conj_product(first, second):
+        return (
+            first[0] * second[0] + first[1] * second[1],
+            first[0] * second[1] - first[1] * second[0],
+        )
+
+    def step_rows(i, kind):
+        wait_bytes(recv_gx.at[i, kind, pl.ds(0, devices - 1)], gx_sem.at[1, 2 * i + kind])
+        exact = jnp.concatenate(
+            [
+                recv_gx[i, kind, b * parts:(b + 1) * parts].reshape(half, LANES)
+                for b in range(groups)
+            ],
+            axis=1,
+        ).astype(jnp.bfloat16)
+        return dot(outer_ref[...], jnp.concatenate([exact, exact], axis=0))
+
+    def held_by(i, b):
+        return filter_grad_ref.at[pl.ds(i * devices + b * parts, parts)]
+
+    def relay(i):
+        wait_bytes(
+            filter_grad_ref.at[pl.ds(i * devices, parts - 1)], filter_grad_sem.at[1, i]
+        )
+        for lead in range(1, groups):
+            remote(
+                held_by(i, group), held_by(i, group), relay_sem, i, after(group, lead, groups), part
+            )
+
     for i in range(count):
+        channel = i * devices + me
         wait_bytes(recv_f.at[i, pl.ds(0, parts - 1)], f_sem.at[1, i])
-        wait_bytes(recv_gx.at[i, pl.ds(0, devices - 1)], gx_sem.at[1, i])
-
-        def signal(kind, b):
-            return recv_gx[i, b * parts:(b + 1) * parts, kind].reshape(half, LANES).astype(jnp.bfloat16)
-
-        exact = jnp.concatenate(
-            [signal(0, b) for b in range(groups)] + [signal(1, b) for b in range(groups)], axis=1
-        )
         high, low = split(recv_f[i].reshape(half, LANES))
-        stepped = dot(outer_ref[...], jnp.concatenate([exact, exact], axis=0))
         filter_part = dot(outer3_ref[...], jnp.concatenate([high, high, low], axis=0))
-        stepped = jnp.concatenate([stepped, filter_part], axis=1)
-        turned = []
-        for s in range(2 * groups + 1):
-            lanes = slice(s * LANES, (s + 1) * LANES)
-            pair = turn(stepped[:half, lanes], stepped[half:, lanes], phi_ref[1])
-            turned.append(jnp.concatenate(pair, axis=1))
-        spec = product3(split(jnp.concatenate(turned, axis=0)), (inner_ref[0], inner_ref[1]))
-
-        def piece(s):
-            block = spec[s * half:(s + 1) * half]
-            return block[:, :LANES], block[:, LANES:]
-
-        filter_spec = piece(2 * groups)
-        products = []
-        total = None
+        *grad_specs, filter_spec = forward(
+            jnp.concatenate([step_rows(i, 0), filter_part], axis=1)
+        )
+        through = backward([conj_product(filter_spec, spec) for spec in grad_specs])
         for b in range(groups):
-            grad_spec, input_spec = piece(b), piece(groups + b)
-            for first in (filter_spec, input_spec):
-                term = jnp.concatenate(
-                    [
-                        first[0] * grad_spec[0] + first[1] * grad_spec[1],
-                        first[0] * grad_spec[1] - first[1] * grad_spec[0],
-                    ],
-                    axis=1,
-                )
-                if first is filter_spec:
-                    products.append(term)
-                else:
-                    total = term if total is None else total + term
-        products.append(total)
-        folded = product3(split(jnp.concatenate(products, axis=0)), (inner_t_ref[0], inner_t_ref[1]))
-        turned = []
-        for s in range(groups + 1):
-            block = folded[s * half:(s + 1) * half]
-            pair = turn(block[:, :LANES], block[:, LANES:], -phi_ref[1])
-            turned.append(jnp.concatenate(pair, axis=0))
-        final = product3((back_ref[0], back_ref[1]), split(jnp.concatenate(turned, axis=1)))
-        send_filter_grad[i] = final[:, groups * LANES:].reshape(parts, rows, LANES)
-        for b in range(groups):
-            through = final[:, b * LANES:(b + 1) * LANES]
-            send_through[i, b * parts:(b + 1) * parts] = through.reshape(parts, rows, LANES)
-
-        channel = i * devices + me
+            send_through[i, b * parts:(b + 1) * parts] = through[b]
+        each_other(
+            lambda to_group, to_part: remote(
+                send_through.at[i, to_group * parts + to_part], through_ref.at[channel],
+                through_sem, i, to_group, to_part,
+            )
+        )
+        through_ref[channel] = send_through[i, me]
+        if i:
+            relay(i - 1)
+
+        terms = [
+            conj_product(first, second)
+            for first, second in zip(forward(step_rows(i, 1)), grad_specs)
+        ]
+        total = (sum(term[0] for term in terms), sum(term[1] for term in terms))
+        send_filter_grad[i] = backward([total])[0]
 
         @pl.loop(1, parts)
         def _(step):
@@ -263,30 +283,13 @@
                 filter_grad_sem, i, group, other,
             )
 
-        each_other(
-            lambda to_group, to_part: remote(
-                send_through.at[i, to_group * parts + to_part], through_ref.at[channel],
-                through_sem, i, to_group, to_part,
-            )
-        )
         filter_grad_ref[channel] = send_filter_grad[i, part]
-        through_ref[channel] = send_through[i, me]
-
-    def held_by(i, b):
-        return filter_grad_ref.at[pl.ds(i * devices + b * parts, parts)]
-
-    for i in range(count):
-        wait_bytes(
-            filter_grad_ref.at[pl.ds(i * devices, parts - 1)], filter_grad_sem.at[1, i]
-        )
-        for lead in range(1, groups):
-            remote(
-                held_by(i, group), held_by(i, group), relay_sem, i, after(group, lead, groups), part
-            )
+    relay(count - 1)
 
     for i in range(count):
         wait_bytes(send_f.at[i, pl.ds(0, parts - 1)], f_sem.at[0, i])
-        wait_bytes(send_gx.at[i, pl.ds(0, devices - 1)], gx_sem.at[0, i])
+        for kind in range(2):
+            wait_bytes(send_gx.at[i, kind, pl.ds(0, devices - 1)], gx_sem.at[0, 2 * i + kind])
         wait_bytes(send_filter_grad.at[i, pl.ds(0, parts - 1)], filter_grad_sem.at[0, i])
         for side in range(2):
             wait_bytes(send_through.at[i, pl.ds(0, devices - 1)], through_sem.at[side, i])
@@ -301,13 +304,15 @@
     count = channels // devices
     outer, phi, inner, back = dft_tables(parts * width)
     outer_high, outer_low = np_split(outer)
+    inner_high, inner_low = np_split(inner)
+    back_high, back_low = np_split(back)
     tables = (
         np.concatenate([outer_high, outer_low], axis=1),
         np.concatenate([outer_high, outer_low, outer_high], axis=1),
         phi,
-        np.stack(np_split(inner)),
-        np.stack(np_split(inner.T)),
-        np.stack(np_split(back)),
+        np.concatenate([inner_high, inner_high, inner_low]),
+        np.concatenate([inner_high.T, inner_high.T, inner_low.T]),
+        np.concatenate([back_high, back_low, back_high], axis=1),
     )
     tables = tuple(jnp.asarray(t) for t in tables)
     operands = (inputs, cotangent, filters) + tables
@@ -319,14 +324,14 @@
         in_specs=[pl.BlockSpec(memory_space=pltpu.HBM)] * len(operands),
         out_specs=(pl.BlockSpec(memory_space=pltpu.VMEM),) * 2,
         scratch_shapes=[pltpu.VMEM(t.shape, t.dtype) for t in operands] + [
-            pltpu.VMEM((count, devices, 2) + tile, jnp.float32),
+            pltpu.VMEM((count, 2, devices) + tile, jnp.float32),
             pltpu.VMEM((count, devices) + tile, jnp.float32),
-            pltpu.VMEM((count, devices, 2) + tile, jnp.float32),
+            pltpu.VMEM((count, 2, devices) + tile, jnp.float32),
             pltpu.VMEM((count, parts) + tile, jnp.float32),
             pltpu.VMEM((count, devices) + tile, jnp.float32),
             pltpu.VMEM((count, parts) + tile, jnp.float32),
             pltpu.SemaphoreType.DMA((len(operands),)),
-        ] + [pltpu.SemaphoreType.DMA((2, count))] * 5,
+        ] + [pltpu.SemaphoreType.DMA((2, 2 * count))] * 5,
         compiler_params=pltpu.CompilerParams(collective_id=0, has_side_effects=True),
     )(*operands)
     through = through.reshape(channels, width)

time: 35.8 us -> 38.2 us (1.067)
  Pallas kernels: 32.1 us -> 34.6 us
    pallas_call x1, Pallas kernels: 32.1 us -> 34.6 us  [fused_body(): pl.pallas_call(functools.partial(kernel, groups, parts, count, half), out...]
where the time goes in v5:
time: 38.2 us; the launch traced here: 38 us
  Pallas kernels  34.6 us (91%)
  local copies, waits for them, and re-layouts  1.98 us (5%)
  other arithmetic  0.75 us (2%)
  between operations  0.68 us (2%)
    pallas_call x1, Pallas kernels, fused_body(): pl.pallas_call(functools.partial(kernel, groups, parts, count, half), out...  34.6 us
    reshape x1, local copies, waits for them, and re-layouts, fused_body(): through = through.reshape(channels, width)  1.03 us
    unnamed x7, local copies, waits for them, and re-layouts  0.95 us

profile of v5, /device:TPU:0, one launch (start us, length us, event | category | flops | bytes accessed | tf_op | source)
XLA Modules:
  0.0 38.0 jit_solution(5277575697046851995)
XLA Ops:
  0.6 34.6 %shard_map.113 = (f32[64,8,128]{2,1,0:T(8,128)}, f32[64,8,128]{2,1,0:T(8,128)}) custom-call(bf16[1,64,1024]{2,1,0:T(8,128)(2,1)} %x_hbm.1, bf16[1,64,1024]{2,1,0:T(8,128)(2,1)} %g_hbm.1, f32[64,1024]{1,0:T(8,128)} %f_hbm.1, bf16[128,128]{1,0:T(8,128)(2,1)} %constant.12.clone.outer_hbm, bf16[128,192]{1,0:T(8,128)(2,1)} %constant.13.clone.outer3_hbm, ...), custom_call_target="tpu_custom_call" | custom-call | tf_op jit(solution)/shard_map/pallas_call | solution.py:321
  35.3 0.0 copy-start
  35.3 0.0 copy-start.2
  35.3 1.0 %reshape.17 = f32[1,64,1024]{2,1,0:T(8,128)S(1)} reshape(f32[64,8,128]{2,1,0:T(8,128)} %get-tuple-element.4) | data formatting | bytes 524288 | tf_op jit(solution)/shard_map/reshape | solution.py:337
  36.3 0.0 copy-done
  36.3 0.0 copy-done.2
  36.3 0.0 copy-start.1
  36.3 0.8 %add_convert_fusion = bf16[1,64,1024]{2,1,0:T(8,128)(2,1)} fusion(f32[1,64,1024]{2,1,0:T(8,128)S(1)} %reshape.17, bf16[1,64,1024]{2,1,0:T(8,128)(2,1)S(1)} %copy-done, f32[64]{0:T(128)S(1)} %copy-done.2), kind=kLoop, calls=%fused_computation.1 | loop fusion | flops 262144 | bytes 524544 | tf_op jit(solution)/shard_map/convert_element_type | solution.py:339
  37.1 0.2 copy-done.1
  37.3 0.8 %copy.14 = f32[8,8,8,128]{3,1,2,0:T(8,128)} copy(f32[8,8,8,128]{3,2,1,0:T(8,128)S(1)} %bitcast.4) | data formatting | bytes 524288
Async XLA Ops:
  35.3 1.1 %copy-start = (bf16[1,64,1024]{2,1,0:T(8,128)(2,1)S(1)}, bf16[1,64,1024]{2,1,0:T(8,128)(2,1)}, u32[]{:S(2)}) copy-start(bf16[1,64,1024]{2,1,0:T(8,128)(2,1)} %g_hbm.1) | copy-start | bytes 393220
  35.3 1.1 %copy-start.2 = (f32[64]{0:T(128)S(1)}, f32[64]{0:T(128)}, u32[]{:S(2)}) copy-start(f32[64]{0:T(128)} %param.13) | copy-start | bytes 772
  36.3 1.0 %copy-start.1 = (f32[64,8,128]{2,1,0:T(8,128)S(1)}, f32[64,8,128]{2,1,0:T(8,128)}, u32[]{:S(2)}) copy-start(f32[64,8,128]{2,1,0:T(8,128)} %get-tuple-element.5) | copy-start | bytes 786436

commit v6 on v3

--- a/solution.py
+++ b/solution.py
@@ -124,13 +124,14 @@
         moved = position + step
         return jnp.where(moved >= size, moved - size, moved)
 
+    others = [after(part, step, parts) for step in range(parts)]
+
     def each_other(act):
         for lead in range(groups):
             there = after(group, lead, groups)
 
-            @pl.loop(0 if lead else 1, parts)
-            def _(step):
-                act(there, after(part, step, parts))
+            for step in range(0 if lead else 1, parts):
+                act(there, others[step])
 
     barrier = pltpu.get_barrier_semaphore()
     each_other(
@@ -161,9 +162,7 @@
             send_f[i, :, r, :] = f_ref[own, lanes]
 
     def send_rows(i):
-        @pl.loop(1, parts)
-        def _(step):
-            other = after(part, step, parts)
+        for other in others[1:]:
             remote(
                 send_f.at[i, group * parts + other], recv_f.at[i, part], f_sem, i, group, other
             )
@@ -255,9 +254,7 @@
 
         channel = i * devices + me
 
-        @pl.loop(1, parts)
-        def _(step):
-            other = after(part, step, parts)
+        for other in others[1:]:
             remote(
                 send_filter_grad.at[i, other], filter_grad_ref.at[channel],
                 filter_grad_sem, i, group, other,

time: 35.8 us -> 35.7 us (level)
  no operation moved by 1% of the time
where the time goes in v6:
time: 35.7 us; the launch traced here: 35.5 us
  Pallas kernels  32.1 us (90%)
  local copies, waits for them, and re-layouts  1.98 us (6%)
  other arithmetic  0.75 us (2%)
  between operations  0.68 us (2%)
    pallas_call x1, Pallas kernels, fused_body(): pl.pallas_call(functools.partial(kernel, groups, parts, count, half), out...  32.1 us
    reshape x1, local copies, waits for them, and re-layouts, fused_body(): through = through.reshape(channels, width)  1.03 us
    unnamed x7, local copies, waits for them, and re-layouts  0.95 us
    convert_element_type x1, other arithmetic, fused_body(): input_grad.astype(jnp.bfloat16)[None]  0.75 us

profile of v6, /device:TPU:0, one launch (start us, length us, event | category | flops | bytes accessed | tf_op | source)
XLA Modules:
  0.0 35.5 jit_solution(10865533162602296270)
XLA Ops:
  0.6 32.1 %shard_map.113 = (f32[64,8,128]{2,1,0:T(8,128)}, f32[64,8,128]{2,1,0:T(8,128)}) custom-call(bf16[1,64,1024]{2,1,0:T(8,128)(2,1)} %x_hbm.1, bf16[1,64,1024]{2,1,0:T(8,128)(2,1)} %g_hbm.1, f32[64,1024]{1,0:T(8,128)} %f_hbm.1, bf16[128,128]{1,0:T(8,128)(2,1)} %constant.12.clone.outer_hbm, bf16[128,192]{1,0:T(8,128)(2,1)} %constant.13.clone.outer3_hbm, ...), custom_call_target="tpu_custom_call" | custom-call | tf_op jit(solution)/shard_map/pallas_call | solution.py:313
  32.8 0.0 copy-start
  32.8 0.0 copy-start.2
  32.8 1.0 %reshape.17 = f32[1,64,1024]{2,1,0:T(8,128)S(1)} reshape(f32[64,8,128]{2,1,0:T(8,128)} %get-tuple-element.4) | data formatting | bytes 524288 | tf_op jit(solution)/shard_map/reshape | solution.py:329
  33.8 0.0 copy-done
  33.8 0.0 copy-done.2
  33.8 0.0 copy-start.1
  33.8 0.8 %add_convert_fusion = bf16[1,64,1024]{2,1,0:T(8,128)(2,1)} fusion(f32[1,64,1024]{2,1,0:T(8,128)S(1)} %reshape.17, bf16[1,64,1024]{2,1,0:T(8,128)(2,1)S(1)} %copy-done, f32[64]{0:T(128)S(1)} %copy-done.2), kind=kLoop, calls=%fused_computation.1 | loop fusion | flops 262144 | bytes 524544 | tf_op jit(solution)/shard_map/convert_element_type | solution.py:331
  34.6 0.2 copy-done.1
  34.8 0.8 %copy.14 = f32[8,8,8,128]{3,1,2,0:T(8,128)} copy(f32[8,8,8,128]{3,2,1,0:T(8,128)S(1)} %bitcast.4) | data formatting | bytes 524288
Async XLA Ops:
  32.8 1.1 %copy-start = (bf16[1,64,1024]{2,1,0:T(8,128)(2,1)S(1)}, bf16[1,64,1024]{2,1,0:T(8,128)(2,1)}, u32[]{:S(2)}) copy-start(bf16[1,64,1024]{2,1,0:T(8,128)(2,1)} %g_hbm.1) | copy-start | bytes 393220
  32.8 1.1 %copy-start.2 = (f32[64]{0:T(128)S(1)}, f32[64]{0:T(128)}, u32[]{:S(2)}) copy-start(f32[64]{0:T(128)} %param.13) | copy-start | bytes 772
  33.8 1.0 %copy-start.1 = (f32[64,8,128]{2,1,0:T(8,128)S(1)}, f32[64,8,128]{2,1,0:T(8,128)}, u32[]{:S(2)}) copy-start(f32[64,8,128]{2,1,0:T(8,128)} %get-tuple-element.5) | copy-start | bytes 786436

commit v7 on v6

--- a/solution.py
+++ b/solution.py
@@ -99,8 +99,8 @@
     x_hbm, g_hbm, f_hbm, outer_hbm, outer3_hbm, phi_hbm, inner_hbm, inner_t_hbm, back_hbm,
     through_ref, filter_grad_ref,
     x_ref, g_ref, f_ref, outer_ref, outer3_ref, phi_ref, inner_ref, inner_t_ref, back_ref,
-    send_gx, send_f, recv_gx, recv_f, send_through, send_filter_grad,
-    load_sem, gx_sem, f_sem, through_sem, filter_grad_sem, relay_sem,
+    send_gx, send_f, recv_gx, recv_f, send_grads, held_grads,
+    load_sem, gx_sem, f_sem, grads_sem, through_sem, filter_grad_sem,
 ):
     devices = groups * parts
     rows = x_ref.shape[2] // LANES
@@ -247,48 +247,37 @@
             pair = turn(block[:, :LANES], block[:, LANES:], -phi_ref[1])
             turned.append(jnp.concatenate(pair, axis=0))
         final = product3((back_ref[0], back_ref[1]), split(jnp.concatenate(turned, axis=1)))
-        send_filter_grad[i] = final[:, groups * LANES:].reshape(parts, rows, LANES)
-        for b in range(groups):
-            through = final[:, b * LANES:(b + 1) * LANES]
-            send_through[i, b * parts:(b + 1) * parts] = through.reshape(parts, rows, LANES)
-
-        channel = i * devices + me
-
+        for b in range(groups + 1):
+            gradient = final[:, b * LANES:(b + 1) * LANES]
+            send_grads[i, :, b] = gradient.reshape(parts, rows, LANES)
         for other in others[1:]:
+            remote(send_grads.at[i, other], held_grads.at[i, part], grads_sem, i, group, other)
+        held_grads[i, part] = send_grads[i, part]
+
+    for i in range(count):
+        own = pl.ds(i * devices + group * parts, parts)
+        wait_bytes(held_grads.at[i, pl.ds(0, parts - 1)], grads_sem.at[1, i])
+        for lead in range(1, groups):
+            there = after(group, lead, groups)
             remote(
-                send_filter_grad.at[i, other], filter_grad_ref.at[channel],
-                filter_grad_sem, i, group, other,
+                held_grads.at[i, pl.ds(0, parts), there], through_ref.at[own],
+                through_sem, i, there, part,
             )
-
-        each_other(
-            lambda to_group, to_part: remote(
-                send_through.at[i, to_group * parts + to_part], through_ref.at[channel],
-                through_sem, i, to_group, to_part,
+            remote(
+                held_grads.at[i, pl.ds(0, parts), groups], filter_grad_ref.at[own],
+                filter_grad_sem, i, there, part,
             )
-        )
-        filter_grad_ref[channel] = send_filter_grad[i, part]
-        through_ref[channel] = send_through[i, me]
-
-    def held_by(i, b):
-        return filter_grad_ref.at[pl.ds(i * devices + b * parts, parts)]
-
-    for i in range(count):
-        wait_bytes(
-            filter_grad_ref.at[pl.ds(i * devices, parts - 1)], filter_grad_sem.at[1, i]
-        )
-        for lead in range(1, groups):
-            remote(
-                held_by(i, group), held_by(i, group), relay_sem, i, after(group, lead, groups), part
-            )
+        through_ref[own] = held_grads[i, :, group]
+        filter_grad_ref[own] = held_grads[i, :, groups]
 
     for i in range(count):
         wait_bytes(send_f.at[i, pl.ds(0, parts - 1)], f_sem.at[0, i])
         wait_bytes(send_gx.at[i, pl.ds(0, devices - 1)], gx_sem.at[0, i])
-        wait_bytes(send_filter_grad.at[i, pl.ds(0, parts - 1)], filter_grad_sem.at[0, i])
+        wait_bytes(send_grads.at[i, pl.ds(0, parts - 1)], grads_sem.at[0, i])
+        others_rows = pl.ds(i * devices, (groups - 1) * parts)
         for side in range(2):
-            wait_bytes(send_through.at[i, pl.ds(0, devices - 1)], through_sem.at[side, i])
-            relayed = pl.ds(i * devices, (groups - 1) * parts)
-            wait_bytes(filter_grad_ref.at[relayed], relay_sem.at[side, i])
+            wait_bytes(through_ref.at[others_rows], through_sem.at[side, i])
+            wait_bytes(filter_grad_ref.at[others_rows], filter_grad_sem.at[side, i])
 
 
 def fused_body(groups, parts, inputs, cotangent, filters, skip_gain):
@@ -320,8 +309,8 @@
             pltpu.VMEM((count, devices) + tile, jnp.float32),
             pltpu.VMEM((count, devices, 2) + tile, jnp.float32),
             pltpu.VMEM((count, parts) + tile, jnp.float32),
-            pltpu.VMEM((count, devices) + tile, jnp.float32),
-            pltpu.VMEM((count, parts) + tile, jnp.float32),
+            pltpu.VMEM((count, parts, groups + 1) + tile, jnp.float32),
+            pltpu.VMEM((count, parts, groups + 1) + tile, jnp.float32),
             pltpu.SemaphoreType.DMA((len(operands),)),
         ] + [pltpu.SemaphoreType.DMA((2, count))] * 5,
         compiler_params=pltpu.CompilerParams(collective_id=0, has_side_effects=True),

time: 35.7 us -> 37.5 us (1.050)
  Pallas kernels: 32.1 us -> 33.9 us
    pallas_call x1, Pallas kernels: 32.1 us -> 33.9 us  [fused_body(): pl.pallas_call(functools.partial(kernel, groups, parts, count, half), out...]
where the time goes in v7:
time: 37.5 us; the launch traced here: 37.3 us
  Pallas kernels  33.9 us (90%)
  local copies, waits for them, and re-layouts  1.98 us (5%)
  other arithmetic  0.75 us (2%)
  between operations  0.68 us (2%)
    pallas_call x1, Pallas kernels, fused_body(): pl.pallas_call(functools.partial(kernel, groups, parts, count, half), out...  33.9 us
    reshape x1, local copies, waits for them, and re-layouts, fused_body(): through = through.reshape(channels, width)  1.03 us
    unnamed x7, local copies, waits for them, and re-layouts  0.95 us
    convert_element_type x1, other arithmetic, fused_body(): input_grad.astype(jnp.bfloat16)[None]  0.75 us

profile of v7, /device:TPU:0, one launch (start us, length us, event | category | flops | bytes accessed | tf_op | source)
XLA Modules:
  0.0 37.3 jit_solution(17439899937735283792)
XLA Ops:
  0.6 33.9 %shard_map.113 = (f32[64,8,128]{2,1,0:T(8,128)}, f32[64,8,128]{2,1,0:T(8,128)}) custom-call(bf16[1,64,1024]{2,1,0:T(8,128)(2,1)} %x_hbm.1, bf16[1,64,1024]{2,1,0:T(8,128)(2,1)} %g_hbm.1, f32[64,1024]{1,0:T(8,128)} %f_hbm.1, bf16[128,128]{1,0:T(8,128)(2,1)} %constant.12.clone.outer_hbm, bf16[128,192]{1,0:T(8,128)(2,1)} %constant.13.clone.outer3_hbm, ...), custom_call_target="tpu_custom_call" | custom-call | tf_op jit(solution)/shard_map/pallas_call | solution.py:302
  34.5 0.0 copy-start
  34.5 0.0 copy-start.2
  34.5 1.0 %reshape.17 = f32[1,64,1024]{2,1,0:T(8,128)S(1)} reshape(f32[64,8,128]{2,1,0:T(8,128)} %get-tuple-element.4) | data formatting | bytes 524288 | tf_op jit(solution)/shard_map/reshape | solution.py:318
  35.6 0.0 copy-done
  35.6 0.0 copy-done.2
  35.6 0.0 copy-start.1
  35.6 0.8 %add_convert_fusion = bf16[1,64,1024]{2,1,0:T(8,128)(2,1)} fusion(f32[1,64,1024]{2,1,0:T(8,128)S(1)} %reshape.17, bf16[1,64,1024]{2,1,0:T(8,128)(2,1)S(1)} %copy-done, f32[64]{0:T(128)S(1)} %copy-done.2), kind=kLoop, calls=%fused_computation.1 | loop fusion | flops 262144 | bytes 524544 | tf_op jit(solution)/shard_map/convert_element_type | solution.py:320
  36.4 0.2 copy-done.1
  36.6 0.8 %copy.14 = f32[8,8,8,128]{3,1,2,0:T(8,128)} copy(f32[8,8,8,128]{3,2,1,0:T(8,128)S(1)} %bitcast.4) | data formatting | bytes 524288
Async XLA Ops:
  34.5 1.1 %copy-start = (bf16[1,64,1024]{2,1,0:T(8,128)(2,1)S(1)}, bf16[1,64,1024]{2,1,0:T(8,128)(2,1)}, u32[]{:S(2)}) copy-start(bf16[1,64,1024]{2,1,0:T(8,128)(2,1)} %g_hbm.1) | copy-start | bytes 393220
  34.5 1.1 %copy-start.2 = (f32[64]{0:T(128)S(1)}, f32[64]{0:T(128)}, u32[]{:S(2)}) copy-start(f32[64]{0:T(128)} %param.13) | copy-start | bytes 772
  35.6 1.0 %copy-start.1 = (f32[64,8,128]{2,1,0:T(8,128)S(1)}, f32[64,8,128]{2,1,0:T(8,128)}, u32[]{:S(2)}) copy-start(f32[64,8,128]{2,1,0:T(8,128)} %get-tuple-element.5) | copy-start | bytes 786436

commit v8 on v5

--- a/solution.py
+++ b/solution.py
@@ -124,13 +124,14 @@
         moved = position + step
         return jnp.where(moved >= size, moved - size, moved)
 
+    others = [after(part, step, parts) for step in range(parts)]
+
     def each_other(act):
         for lead in range(groups):
             there = after(group, lead, groups)
 
-            @pl.loop(0 if lead else 1, parts)
-            def _(step):
-                act(there, after(part, step, parts))
+            for step in range(0 if lead else 1, parts):
+                act(there, others[step])
 
     barrier = pltpu.get_barrier_semaphore()
     each_other(
@@ -139,12 +140,12 @@
         )
     )
 
-    def remote(source, target, sems, i, to_group, to_part):
+    def remote(source, target, sems, to_group, to_part):
         pltpu.make_async_remote_copy(
             src_ref=source,
             dst_ref=target,
-            send_sem=sems.at[0, i],
-            recv_sem=sems.at[1, i],
+            send_sem=sems.at[0],
+            recv_sem=sems.at[1],
             device_id=(to_group, to_part),
             device_id_type=MESH,
         ).start()
@@ -153,54 +154,46 @@
         pltpu.make_async_copy(held, held, sem).wait()
 
     def pack(target, source):
-        for r in range(rows):
-            target[:, r, :] = source[:, r * LANES:(r + 1) * LANES].astype(jnp.float32)
-
-    def send_filters(i):
-        @pl.loop(1, parts)
-        def _(step):
-            other = after(part, step, parts)
-            remote(
-                send_f.at[i, group * parts + other], recv_f.at[i, part], f_sem, i, group, other
-            )
-
-        recv_f[i, part] = send_f[i, me]
-
-    def send_rows(i, kind):
+        for i in range(count):
+            for r in range(rows):
+                block = source[i * devices:(i + 1) * devices, r * LANES:(r + 1) * LANES]
+                target[:, i, r, :] = block.astype(jnp.float32)
+
+    def send_rows(kind):
         each_other(
             lambda to_group, to_part: remote(
-                send_gx.at[i, kind, to_group * parts + to_part], recv_gx.at[i, kind, me],
-                gx_sem, 2 * i + kind, to_group, to_part,
+                send_gx.at[kind, to_group * parts + to_part], recv_gx.at[kind, me],
+                gx_sem.at[kind], to_group, to_part,
             )
         )
-        recv_gx[i, kind, me] = send_gx[i, kind, me]
-
-    for i in range(count):
-        own = slice(i * devices, (i + 1) * devices)
-        for kind, source in enumerate((g_ref, x_ref)):
-            if i == 0:
-                loads[kind].wait()
-            if kind == 0:
-                if i == 0:
-                    loads[2].wait()
-                pack(send_f.at[i], f_ref.at[own])
-            pack(send_gx.at[i, kind], source.at[0, own])
-            if i == 0 and kind == 0:
-                pl.semaphore_wait(barrier, devices - 1)
-            if kind == 0:
-                send_filters(i)
-            send_rows(i, kind)
+        recv_gx[kind, me] = send_gx[kind, me]
+
+    loads[2].wait()
+    pack(send_f, f_ref)
+    pl.semaphore_wait(barrier, devices - 1)
+    for other in others[1:]:
+        remote(send_f.at[group * parts + other], recv_f.at[part], f_sem, group, other)
+    recv_f[part] = send_f[me]
+    for kind, source in enumerate((g_ref, x_ref)):
+        loads[kind].wait()
+        pack(send_gx.at[kind], source.at[0])
+        send_rows(kind)
     for load in loads[3:]:
         load.wait()
+
+    def product3(left, right):
+        (left_high, left_low), (right_high, right_low) = left, right
+        return (
+            dot(left_high, right_high) + dot(left_low, right_high) + dot(left_high, right_low)
+        )
 
     def turn(real, imag, sine):
         cosine = phi_ref[0]
         return real * cosine - imag * sine, real * sine + imag * cosine
 
     def along_lanes(pairs, table_ref):
-        values = jnp.concatenate([jnp.concatenate(pair, axis=1) for pair in pairs], axis=0)
-        high, low = split(values)
-        out = dot(jnp.concatenate([high, low, high], axis=1), table_ref[...])
+        rows_in = jnp.concatenate([jnp.concatenate(pair, axis=1) for pair in pairs], axis=0)
+        out = product3(split(rows_in), (table_ref[0], table_ref[1]))
         blocks = [out[s * half:(s + 1) * half] for s in range(len(pairs))]
         return [(block[:, :LANES], block[:, LANES:]) for block in blocks]
 
@@ -211,9 +204,8 @@
 
     def backward(specs):
         pairs = [turn(real, imag, -phi_ref[1]) for real, imag in along_lanes(specs, inner_t_ref)]
-        values = jnp.concatenate([jnp.concatenate(pair, axis=0) for pair in pairs], axis=1)
-        high, low = split(values)
-        out = dot(back_ref[...], jnp.concatenate([high, high, low], axis=0))
+        turned = jnp.concatenate([jnp.concatenate(pair, axis=0) for pair in pairs], axis=1)
+        out = product3((back_ref[0], back_ref[1]), split(turned))
         return [
             out[:, s:s + LANES].reshape(parts, rows, LANES) for s in range(0, out.shape[1], LANES)
         ]
@@ -224,77 +216,67 @@
             first[0] * second[1] - first[1] * second[0],
         )
 
-    def step_rows(i, kind):
-        wait_bytes(recv_gx.at[i, kind, pl.ds(0, devices - 1)], gx_sem.at[1, 2 * i + kind])
+    def step_rows(kind):
+        wait_bytes(recv_gx.at[kind, pl.ds(0, devices - 1)], gx_sem.at[kind, 1])
         exact = jnp.concatenate(
             [
-                recv_gx[i, kind, b * parts:(b + 1) * parts].reshape(half, LANES)
+                recv_gx[kind, b * parts:(b + 1) * parts, i].reshape(half, LANES)
+                for i in range(count)
                 for b in range(groups)
             ],
             axis=1,
         ).astype(jnp.bfloat16)
         return dot(outer_ref[...], jnp.concatenate([exact, exact], axis=0))
 
-    def held_by(i, b):
-        return filter_grad_ref.at[pl.ds(i * devices + b * parts, parts)]
-
-    def relay(i):
-        wait_bytes(
-            filter_grad_ref.at[pl.ds(i * devices, parts - 1)], filter_grad_sem.at[1, i]
-        )
-        for lead in range(1, groups):
-            remote(
-                held_by(i, group), held_by(i, group), relay_sem, i, after(group, lead, groups), part
-            )
-
+    both = pl.ds(0, count)
+    wait_bytes(recv_f.at[pl.ds(0, parts - 1)], f_sem.at[1])
+    high, low = split(
+        jnp.concatenate([recv_f[:, i].reshape(half, LANES) for i in range(count)], axis=1)
+    )
+    filter_part = dot(outer3_ref[...], jnp.concatenate([high, high, low], axis=0))
+    specs = forward(jnp.concatenate([step_rows(0), filter_part], axis=1))
+    grad_specs, filter_specs = specs[:count * groups], specs[count * groups:]
+    through = backward(
+        [conj_product(filter_specs[s // groups], spec) for s, spec in enumerate(grad_specs)]
+    )
+    for s, tiles in enumerate(through):
+        i, b = s // groups, s % groups
+        send_through[b * parts:(b + 1) * parts, i] = tiles
+    each_other(
+        lambda to_group, to_part: remote(
+            send_through.at[to_group * parts + to_part], through_ref.at[both, me],
+            through_sem, to_group, to_part,
+        )
+    )
+    through_ref[:, me] = send_through[me]
+
+    terms = [
+        conj_product(first, second) for first, second in zip(forward(step_rows(1)), grad_specs)
+    ]
+    totals = []
     for i in range(count):
-        channel = i * devices + me
-        wait_bytes(recv_f.at[i, pl.ds(0, parts - 1)], f_sem.at[1, i])
-        high, low = split(recv_f[i].reshape(half, LANES))
-        filter_part = dot(outer3_ref[...], jnp.concatenate([high, high, low], axis=0))
-        *grad_specs, filter_spec = forward(
-            jnp.concatenate([step_rows(i, 0), filter_part], axis=1)
-        )
-        through = backward([conj_product(filter_spec, spec) for spec in grad_specs])
-        for b in range(groups):
-            send_through[i, b * parts:(b + 1) * parts] = through[b]
-        each_other(
-            lambda to_group, to_part: remote(
-                send_through.at[i, to_group * parts + to_part], through_ref.at[channel],
-                through_sem, i, to_group, to_part,
-            )
-        )
-        through_ref[channel] = send_through[i, me]
-        if i:
-            relay(i - 1)
-
-        terms = [
-            conj_product(first, second)
-            for first, second in zip(forward(step_rows(i, 1)), grad_specs)
-        ]
-        total = (sum(term[0] for term in terms), sum(term[1] for term in terms))
-        send_filter_grad[i] = backward([total])[0]
-
-        @pl.loop(1, parts)
-        def _(step):
-            other = after(part, step, parts)
-            remote(
-                send_filter_grad.at[i, other], filter_grad_ref.at[channel],
-                filter_grad_sem, i, group, other,
-            )
-
-        filter_grad_ref[channel] = send_filter_grad[i, part]
-    relay(count - 1)
-
-    for i in range(count):
-        wait_bytes(send_f.at[i, pl.ds(0, parts - 1)], f_sem.at[0, i])
-        for kind in range(2):
-            wait_bytes(send_gx.at[i, kind, pl.ds(0, devices - 1)], gx_sem.at[0, 2 * i + kind])
-        wait_bytes(send_filter_grad.at[i, pl.ds(0, parts - 1)], filter_grad_sem.at[0, i])
-        for side in range(2):
-            wait_bytes(send_through.at[i, pl.ds(0, devices - 1)], through_sem.at[side, i])
-            relayed = pl.ds(i * devices, (groups - 1) * parts)
-            wait_bytes(filter_grad_ref.at[relayed], relay_sem.at[side, i])
+        real, imag = zip(*terms[i * groups:(i + 1) * groups])
+        totals.append((sum(real[1:], real[0]), sum(imag[1:], imag[0])))
+    for i, tiles in enumerate(backward(totals)):
+        send_filter_grad[:, i] = tiles
+    for other in others[1:]:
+        remote(
+            send_filter_grad.at[other], filter_grad_ref.at[both, me], filter_grad_sem, group, other
+        )
+    filter_grad_ref[:, me] = send_filter_grad[part]
+
+    own = filter_grad_ref.at[both, pl.ds(group * parts, parts)]
+    wait_bytes(filter_grad_ref.at[both, pl.ds(0, parts - 1)], filter_grad_sem.at[1])
+    for lead in range(1, groups):
+        remote(own, own, relay_sem, after(group, lead, groups), part)
+
+    wait_bytes(send_f.at[pl.ds(0, parts - 1)], f_sem.at[0])
+    for kind in range(2):
+        wait_bytes(send_gx.at[kind, pl.ds(0, devices - 1)], gx_sem.at[kind, 0])
+    wait_bytes(send_filter_grad.at[pl.ds(0, parts - 1)], filter_grad_sem.at[0])
+    for side in range(2):
+        wait_bytes(send_through.at[pl.ds(0, devices - 1)], through_sem.at[side])
+        wait_bytes(filter_grad_ref.at[both, pl.ds(0, (groups - 1) * parts)], relay_sem.at[side])
 
 
 def fused_body(groups, parts, inputs, cotangent, filters, skip_gain):
@@ -304,34 +286,33 @@
     count = channels // devices
     outer, phi, inner, back = dft_tables(parts * width)
     outer_high, outer_low = np_split(outer)
-    inner_high, inner_low = np_split(inner)
-    back_high, back_low = np_split(back)
     tables = (
         np.concatenate([outer_high, outer_low], axis=1),
         np.concatenate([outer_high, outer_low, outer_high], axis=1),
         phi,
-        np.concatenate([inner_high, inner_high, inner_low]),
-        np.concatenate([inner_high.T, inner_high.T, inner_low.T]),
-        np.concatenate([back_high, back_low, back_high], axis=1),
+        np.stack(np_split(inner)),
+        np.stack(np_split(inner.T)),
+        np.stack(np_split(back)),
     )
     tables = tuple(jnp.asarray(t) for t in tables)
     operands = (inputs, cotangent, filters) + tables
     tile = (rows, LANES)
-    whole = jax.ShapeDtypeStruct((channels,) + tile, jnp.float32)
+    whole = jax.ShapeDtypeStruct((count, devices) + tile, jnp.float32)
     through, filter_grad = pl.pallas_call(
         functools.partial(kernel, groups, parts, count, half),
         out_shape=(whole, whole),
         in_specs=[pl.BlockSpec(memory_space=pltpu.HBM)] * len(operands),
         out_specs=(pl.BlockSpec(memory_space=pltpu.VMEM),) * 2,
         scratch_shapes=[pltpu.VMEM(t.shape, t.dtype) for t in operands] + [
-            pltpu.VMEM((count, 2, devices) + tile, jnp.float32),
-            pltpu.VMEM((count, devices) + tile, jnp.float32),
-            pltpu.VMEM((count, 2, devices) + tile, jnp.float32),
-            pltpu.VMEM((count, parts) + tile, jnp.float32),
-            pltpu.VMEM((count, devices) + tile, jnp.float32),
-            pltpu.VMEM((count, parts) + tile, jnp.float32),
+            pltpu.VMEM((2, devices, count) + tile, jnp.float32),
+            pltpu.VMEM((devices, count) + tile, jnp.float32),
+            pltpu.VMEM((2, devices, count) + tile, jnp.float32),
+            pltpu.VMEM((parts, count) + tile, jnp.float32),
+            pltpu.VMEM((devices, count) + tile, jnp.float32),
+            pltpu.VMEM((parts, count) + tile, jnp.float32),
             pltpu.SemaphoreType.DMA((len(operands),)),
-        ] + [pltpu.SemaphoreType.DMA((2, 2 * count))] * 5,
+            pltpu.SemaphoreType.DMA((2, 2)),
+        ] + [pltpu.SemaphoreType.DMA((2,))] * 4,
         compiler_params=pltpu.CompilerParams(collective_id=0, has_side_effects=True),
     )(*operands)
     through = through.reshape(channels, width)

time: 38.2 us -> 37.7 us (0.987)
  Pallas kernels: 34.6 us -> 34.1 us
    pallas_call x1, Pallas kernels: 34.6 us -> 34.1 us  [fused_body(): pl.pallas_call(functools.partial(kernel, groups, parts, count, half), out...]
where the time goes in v8:
time: 37.7 us; the launch traced here: 37.5 us
  Pallas kernels  34.1 us (90%)
  local copies, waits for them, and re-layouts  1.98 us (5%)
  other arithmetic  0.75 us (2%)
  between operations  0.68 us (2%)
    pallas_call x1, Pallas kernels, fused_body(): pl.pallas_call(functools.partial(kernel, groups, parts, count, half), out...  34.1 us
    reshape x1, local copies, waits for them, and re-layouts, fused_body(): through = through.reshape(channels, width)  1.03 us
    unnamed x7, local copies, waits for them, and re-layouts  0.95 us
    convert_element_type x1, other arithmetic, fused_body(): input_grad.astype(jnp.bfloat16)[None]  0.75 us

profile of v8, /device:TPU:0, one launch (start us, length us, event | category | flops | bytes accessed | tf_op | source)
XLA Modules:
  0.0 37.5 jit_solution(16558722932976614304)
XLA Ops:
  0.6 34.1 %shard_map.113 = (f32[2,32,8,128]{3,2,1,0:T(8,128)}, f32[2,32,8,128]{3,2,1,0:T(8,128)}) custom-call(bf16[1,64,1024]{2,1,0:T(8,128)(2,1)} %x_hbm.1, bf16[1,64,1024]{2,1,0:T(8,128)(2,1)} %g_hbm.1, f32[64,1024]{1,0:T(8,128)} %f_hbm.1, bf16[128,128]{1,0:T(8,128)(2,1)} %constant.12.clone.outer_hbm, bf16[128,192]{1,0:T(8,128)(2,1)} %constant.13.clone.outer3_hbm, ...), custom_call_target="tpu_custom_call" | custom-call | tf_op jit(solution)/shard_map/pallas_call | solution.py:301
  34.7 0.0 copy-start
  34.7 0.0 copy-start.2
  34.8 1.0 %reshape.17 = f32[1,64,1024]{2,1,0:T(8,128)S(1)} reshape(f32[2,32,8,128]{3,2,1,0:T(8,128)} %get-tuple-element.4) | data formatting | bytes 524288 | tf_op jit(solution)/shard_map/reshape | solution.py:318
  35.8 0.0 copy-done
  35.8 0.0 copy-done.2
  35.8 0.0 copy-start.1
  35.8 0.8 %add_convert_fusion = bf16[1,64,1024]{2,1,0:T(8,128)(2,1)} fusion(f32[1,64,1024]{2,1,0:T(8,128)S(1)} %reshape.17, bf16[1,64,1024]{2,1,0:T(8,128)(2,1)S(1)} %copy-done, f32[64]{0:T(128)S(1)} %copy-done.2), kind=kLoop, calls=%fused_computation.1 | loop fusion | flops 262144 | bytes 524544 | tf_op jit(solution)/shard_map/convert_element_type | solution.py:320
  36.6 0.2 copy-done.1
  36.8 0.8 %copy.14 = f32[8,8,8,128]{3,1,2,0:T(8,128)} copy(f32[8,8,8,128]{3,2,1,0:T(8,128)S(1)} %bitcast.7) | data formatting | bytes 524288
Async XLA Ops:
  34.7 1.1 %copy-start = (bf16[1,64,1024]{2,1,0:T(8,128)(2,1)S(1)}, bf16[1,64,1024]{2,1,0:T(8,128)(2,1)}, u32[]{:S(2)}) copy-start(bf16[1,64,1024]{2,1,0:T(8,128)(2,1)} %g_hbm.1) | copy-start | bytes 393220
  34.7 1.1 %copy-start.2 = (f32[64]{0:T(128)S(1)}, f32[64]{0:T(128)}, u32[]{:S(2)}) copy-start(f32[64]{0:T(128)} %param.13) | copy-start | bytes 772
  35.8 1.0 %copy-start.1 = (f32[2,32,8,128]{3,2,1,0:T(8,128)S(1)}, f32[2,32,8,128]{3,2,1,0:T(8,128)}, u32[]{:S(2)}) copy-start(f32[2,32,8,128]{3,2,1,0:T(8,128)} %get-tuple-element.5) | copy-start | bytes 786436

commit v9 on v6

--- a/solution.py
+++ b/solution.py
@@ -97,9 +97,12 @@
 def kernel(
     groups, parts, count, half,
     x_hbm, g_hbm, f_hbm, outer_hbm, outer3_hbm, phi_hbm, inner_hbm, inner_t_hbm, back_hbm,
-    through_ref, filter_grad_ref,
+    skip_hbm,
+    input_grad_ref, filter_grad_ref,
     x_ref, g_ref, f_ref, outer_ref, outer3_ref, phi_ref, inner_ref, inner_t_ref, back_ref,
+    skip_ref,
     send_gx, send_f, recv_gx, recv_f, send_through, send_filter_grad,
+    through_got, filter_grad_got,
     load_sem, gx_sem, f_sem, through_sem, filter_grad_sem, relay_sem,
 ):
     devices = groups * parts
@@ -114,6 +117,7 @@
                 (g_hbm, g_ref), (x_hbm, x_ref), (f_hbm, f_ref),
                 (outer_hbm, outer_ref), (outer3_hbm, outer3_ref), (phi_hbm, phi_ref),
                 (inner_hbm, inner_ref), (inner_t_hbm, inner_t_ref), (back_hbm, back_ref),
+                (skip_hbm, skip_ref),
             ]
         )
     ]
@@ -207,88 +211,99 @@
         exact = jnp.concatenate(
             [signal(0, b) for b in range(groups)] + [signal(1, b) for b in range(groups)], axis=1
         )
-        high, low = split(recv_f[i].reshape(half, LANES))
-        stepped = dot(outer_ref[...], jnp.concatenate([exact, exact], axis=0))
-        filter_part = dot(outer3_ref[...], jnp.concatenate([high, high, low], axis=0))
-        stepped = jnp.concatenate([stepped, filter_part], axis=1)
-        turned = []
-        for s in range(2 * groups + 1):
-            lanes = slice(s * LANES, (s + 1) * LANES)
-            pair = turn(stepped[:half, lanes], stepped[half:, lanes], phi_ref[1])
-            turned.append(jnp.concatenate(pair, axis=1))
-        spec = product3(split(jnp.concatenate(turned, axis=0)), (inner_ref[0], inner_ref[1]))
-
-        def piece(s):
-            block = spec[s * half:(s + 1) * half]
-            return block[:, :LANES], block[:, LANES:]
-
-        filter_spec = piece(2 * groups)
-        products = []
-        total = None
-        for b in range(groups):
-            grad_spec, input_spec = piece(b), piece(groups + b)
-            for first in (filter_spec, input_spec):
-                term = jnp.concatenate(
-                    [
-                        first[0] * grad_spec[0] + first[1] * grad_spec[1],
-                        first[0] * grad_spec[1] - first[1] * grad_spec[0],
-                    ],
-                    axis=1,
-                )
-                if first is filter_spec:
-                    products.append(term)
-                else:
-                    total = term if total is None else total + term
-        products.append(total)
-        folded = product3(split(jnp.concatenate(products, axis=0)), (inner_t_ref[0], inner_t_ref[1]))
-        turned = []
-        for s in range(groups + 1):
-            block = folded[s * half:(s + 1) * half]
-            pair = turn(block[:, :LANES], block[:, LANES:], -phi_ref[1])
-            turned.append(jnp.concatenate(pair, axis=0))
-        final = product3((back_ref[0], back_ref[1]), split(jnp.concatenate(turned, axis=1)))
-        send_filter_grad[i] = final[:, groups * LANES:].reshape(parts, rows, LANES)
-        for b in range(groups):
-            through = final[:, b * LANES:(b + 1) * LANES]
-            send_through[i, b * parts:(b + 1) * parts] = through.reshape(parts, rows, LANES)
-
+        def forward(stepped):
+            blocks = [stepped[:, k:k + LANES] for k in range(0, stepped.shape[1], LANES)]
+            turned = [
+                jnp.concatenate(turn(block[:half], block[half:], phi_ref[1]), axis=1)
+                for block in blocks
+            ]
+            return pieces(jnp.concatenate(turned, axis=0), inner_ref)
+
+        def pieces(values, table_ref):
+            out = product3(split(values), (table_ref[0], table_ref[1]))
+            blocks = [out[k:k + half] for k in range(0, out.shape[0], half)]
+            return [(block[:, :LANES], block[:, LANES:]) for block in blocks]
+
+        def backward(specs):
+            values = jnp.concatenate([jnp.concatenate(pair, axis=1) for pair in specs], axis=0)
+            turned = [
+                jnp.concatenate(turn(real, imag, -phi_ref[1]), axis=0)
+                for real, imag in pieces(values, inner_t_ref)
+            ]
+            out = product3((back_ref[0], back_ref[1]), split(jnp.concatenate(turned, axis=1)))
+            blocks = [out[:, k:k + LANES] for k in range(0, out.shape[1], LANES)]
+            return [block.reshape(parts, rows, LANES) for block in blocks]
+
+        def conj_product(first, second):
+            return (
+                first[0] * second[0] + first[1] * second[1],
+                first[0] * second[1] - first[1] * second[0],
+            )
+
+        exact = jnp.concatenate(
+            [signal(0, b) for b in range(groups)] + [signal(1, b) for b in range(groups)], axis=1
+        )
+        specs = forward(dot(outer_ref[...], jnp.concatenate([exact, exact], axis=0)))
+        grad_specs, input_specs = specs[:groups], specs[groups:]
+        terms = [conj_product(first, second) for first, second in zip(input_specs, grad_specs)]
+        real, imag = zip(*terms)
+        send_filter_grad[i] = backward([(sum(real[1:], real[0]), sum(imag[1:], imag[0]))])[0]
         channel = i * devices + me
-
         for other in others[1:]:
             remote(
-                send_filter_grad.at[i, other], filter_grad_ref.at[channel],
+                send_filter_grad.at[i, other], filter_grad_got.at[channel],
                 filter_grad_sem, i, group, other,
             )
-
+        filter_grad_got[channel] = send_filter_grad[i, part]
+
+        high, low = split(recv_f[i].reshape(half, LANES))
+        filter_part = dot(outer3_ref[...], jnp.concatenate([high, high, low], axis=0))
+        filter_spec = forward(filter_part)[0]
+        for b, tiles in enumerate(backward([conj_product(filter_spec, g) for g in grad_specs])):
+            send_through[i, b * parts:(b + 1) * parts] = tiles
         each_other(
             lambda to_group, to_part: remote(
-                send_through.at[i, to_group * parts + to_part], through_ref.at[channel],
+                send_through.at[i, to_group * parts + to_part], through_got.at[channel],
                 through_sem, i, to_group, to_part,
             )
         )
-        filter_grad_ref[channel] = send_filter_grad[i, part]
-        through_ref[channel] = send_through[i, me]
+        through_got[channel] = send_through[i, me]
 
     def held_by(i, b):
-        return filter_grad_ref.at[pl.ds(i * devices + b * parts, parts)]
+        return filter_grad_got.at[pl.ds(i * devices + b * parts, parts)]
 
     for i in range(count):
         wait_bytes(
-            filter_grad_ref.at[pl.ds(i * devices, parts - 1)], filter_grad_sem.at[1, i]
+            filter_grad_got.at[pl.ds(i * devices, parts - 1)], filter_grad_sem.at[1, i]
         )
         for lead in range(1, groups):
             remote(
                 held_by(i, group), held_by(i, group), relay_sem, i, after(group, lead, groups), part
             )
+
+    size = skip_ref.shape[1]
+    square = (size, size)
+    on_diagonal = (
+        lax.broadcasted_iota(jnp.int32, square, 0) == lax.broadcasted_iota(jnp.int32, square, 1)
+    )
+    skip = jnp.sum(jnp.where(on_diagonal, skip_ref[...], 0.0), axis=1, keepdims=True)
+    for i in range(count):
+        own = slice(i * devices, (i + 1) * devices)
+        wait_bytes(send_through.at[i, pl.ds(0, devices - 1)], through_sem.at[1, i])
+        for r in range(rows):
+            lanes = slice(r * LANES, (r + 1) * LANES)
+            skipped = skip[own] * g_ref[0, own, lanes].astype(jnp.float32)
+            input_grad_ref[0, own, lanes] = (through_got[own, r, :] + skipped).astype(jnp.bfloat16)
+        wait_bytes(filter_grad_got.at[pl.ds(0, (groups - 1) * parts)], relay_sem.at[1, i])
+        for r in range(rows):
+            filter_grad_ref[own, r * LANES:(r + 1) * LANES] = filter_grad_got[own, r, :]
 
     for i in range(count):
         wait_bytes(send_f.at[i, pl.ds(0, parts - 1)], f_sem.at[0, i])
         wait_bytes(send_gx.at[i, pl.ds(0, devices - 1)], gx_sem.at[0, i])
         wait_bytes(send_filter_grad.at[i, pl.ds(0, parts - 1)], filter_grad_sem.at[0, i])
-        for side in range(2):
-            wait_bytes(send_through.at[i, pl.ds(0, devices - 1)], through_sem.at[side, i])
-            relayed = pl.ds(i * devices, (groups - 1) * parts)
-            wait_bytes(filter_grad_ref.at[relayed], relay_sem.at[side, i])
+        wait_bytes(send_through.at[i, pl.ds(0, devices - 1)], through_sem.at[0, i])
+        wait_bytes(filter_grad_got.at[pl.ds(0, (groups - 1) * parts)], relay_sem.at[0, i])
 
 
 def fused_body(groups, parts, inputs, cotangent, filters, skip_gain):
@@ -307,12 +322,14 @@
         np.stack(np_split(back)),
     )
     tables = tuple(jnp.asarray(t) for t in tables)
-    operands = (inputs, cotangent, filters) + tables
+    operands = (inputs, cotangent, filters) + tables + (skip_gain.reshape(1, channels),)
     tile = (rows, LANES)
-    whole = jax.ShapeDtypeStruct((channels,) + tile, jnp.float32)
-    through, filter_grad = pl.pallas_call(
+    return pl.pallas_call(
         functools.partial(kernel, groups, parts, count, half),
-        out_shape=(whole, whole),
+        out_shape=(
+            jax.ShapeDtypeStruct(cotangent.shape, jnp.bfloat16),
+            jax.ShapeDtypeStruct(filters.shape, jnp.float32),
+        ),
         in_specs=[pl.BlockSpec(memory_space=pltpu.HBM)] * len(operands),
         out_specs=(pl.BlockSpec(memory_space=pltpu.VMEM),) * 2,
         scratch_shapes=[pltpu.VMEM(t.shape, t.dtype) for t in operands] + [
@@ -322,13 +339,12 @@
             pltpu.VMEM((count, parts) + tile, jnp.float32),
             pltpu.VMEM((count, devices) + tile, jnp.float32),
             pltpu.VMEM((count, parts) + tile, jnp.float32),
+            pltpu.VMEM((channels,) + tile, jnp.float32),
+            pltpu.VMEM((channels,) + tile, jnp.float32),
             pltpu.SemaphoreType.DMA((len(operands),)),
         ] + [pltpu.SemaphoreType.DMA((2, count))] * 5,
         compiler_params=pltpu.CompilerParams(collective_id=0, has_side_effects=True),
     )(*operands)
-    through = through.reshape(channels, width)
-    input_grad = through + skip_gain[:, None] * cotangent[0].astype(jnp.float32)
-    return input_grad.astype(jnp.bfloat16)[None], filter_grad.reshape(channels, width)
 
 
 def solution(mesh):

time: 35.7 us -> 35.3 us (0.989)
  other arithmetic: 0.75 us -> 0 us
    unnamed x7 -> x4, local copies, waits for them, and re-layouts: 0.95 us -> 2.32 us
    reshape x1 -> x0, local copies, waits for them, and re-layouts: 1.03 us -> none  [fused_body(): through = through.reshape(channels, width)]
    convert_element_type x1 -> x0, other arithmetic: 0.75 us -> none  [fused_body(): input_grad.astype(jnp.bfloat16)[None]]
where the time goes in v9:
time: 35.3 us; the launch traced here: 35.2 us
  Pallas kernels  32.2 us (91%)
  local copies, waits for them, and re-layouts  2.32 us (7%)
  between operations  0.65 us (2%)
    pallas_call x1, Pallas kernels, fused_body(): pl.pallas_call(functools.partial(kernel, groups, parts, count, half), out...  32.2 us
    unnamed x4, local copies, waits for them, and re-layouts  2.32 us

profile of v9, /device:TPU:0, one launch (start us, length us, event | category | flops | bytes accessed | tf_op | source)
XLA Modules:
  0.0 35.2 jit_solution(3298161140750150383)
XLA Ops:
  0.6 32.2 %shard_map.113 = (bf16[1,64,1024]{2,1,0:T(8,128)(2,1)}, f32[64,1024]{1,0:T(8,128)}) custom-call(bf16[1,64,1024]{2,1,0:T(8,128)(2,1)} %x_hbm.1, bf16[1,64,1024]{2,1,0:T(8,128)(2,1)} %g_hbm.1, f32[64,1024]{1,0:T(8,128)} %f_hbm.1, bf16[128,128]{1,0:T(8,128)(2,1)} %constant.12.clone.outer_hbm, bf16[128,192]{1,0:T(8,128)(2,1)} %constant.13.clone.outer3_hbm, ...), custom_call_target="tpu_custom_call" | custom-call | tf_op jit(solution)/shard_map/pallas_call | solution.py:327
  32.8 0.0 copy-start
  32.8 1.6 %copy.14 = bf16[1,64,1024]{2,1,0:T(8,128)(2,1)} copy(bf16[1,64,1024]{2,1,0:T(8,128)(2,1)} %get-tuple-element.4) | data formatting | bytes 262144
  34.5 0.0 copy-done
  34.5 0.7 %copy.15 = f32[64,1024]{1,0:T(8,128)} copy(f32[64,1024]{1,0:T(8,128)S(1)} %copy-done) | data formatting | bytes 524288
Async XLA Ops:
  32.8 1.6 %copy-start = (f32[64,1024]{1,0:T(8,128)S(1)}, f32[64,1024]{1,0:T(8,128)}, u32[]{:S(2)}) copy-start(f32[64,1024]{1,0:T(8,128)} %get-tuple-element.5) | copy-start | bytes 786436

commit v10 on v9

--- a/solution.py
+++ b/solution.py
@@ -128,14 +128,14 @@
         moved = position + step
         return jnp.where(moved >= size, moved - size, moved)
 
-    others = [after(part, step, parts) for step in range(parts)]
+    steps = sorted(range(parts), key=lambda step: abs(step - parts // 2))
+    others = [after(part, step, parts) for step in steps if step]
+    leads = [after(group, lead, groups) for lead in range(groups)]
 
     def each_other(act):
-        for lead in range(groups):
-            there = after(group, lead, groups)
-
-            for step in range(0 if lead else 1, parts):
-                act(there, others[step])
+        for step in steps:
+            for lead in range(0 if step else 1, groups):
+                act(leads[lead], after(part, step, parts))
 
     barrier = pltpu.get_barrier_semaphore()
     each_other(
@@ -166,7 +166,7 @@
             send_f[i, :, r, :] = f_ref[own, lanes]
 
     def send_rows(i):
-        for other in others[1:]:
+        for other in others:
             remote(
                 send_f.at[i, group * parts + other], recv_f.at[i, part], f_sem, i, group, other
             )
@@ -249,7 +249,7 @@
         real, imag = zip(*terms)
         send_filter_grad[i] = backward([(sum(real[1:], real[0]), sum(imag[1:], imag[0]))])[0]
         channel = i * devices + me
-        for other in others[1:]:
+        for other in others:
             remote(
                 send_filter_grad.at[i, other], filter_grad_got.at[channel],
                 filter_grad_sem, i, group, other,

time: 35.3 us -> 36.6 us (1.037)
  Pallas kernels: 32.2 us -> 33.5 us
    pallas_call x1, Pallas kernels: 32.2 us -> 33.5 us  [fused_body(): pl.pallas_call(functools.partial(kernel, groups, parts, count, half), out...]
where the time goes in v10:
time: 36.6 us; the launch traced here: 36.5 us
  Pallas kernels  33.5 us (92%)
  local copies, waits for them, and re-layouts  2.32 us (6%)
  between operations  0.65 us (2%)
    pallas_call x1, Pallas kernels, fused_body(): pl.pallas_call(functools.partial(kernel, groups, parts, count, half), out...  33.5 us
    unnamed x4, local copies, waits for them, and re-layouts  2.32 us

profile of v10, /device:TPU:0, one launch (start us, length us, event | category | flops | bytes accessed | tf_op | source)
XLA Modules:
  0.0 36.5 jit_solution(8008460190769106227)
XLA Ops:
  0.6 33.5 %shard_map.113 = (bf16[1,64,1024]{2,1,0:T(8,128)(2,1)}, f32[64,1024]{1,0:T(8,128)}) custom-call(bf16[1,64,1024]{2,1,0:T(8,128)(2,1)} %x_hbm.1, bf16[1,64,1024]{2,1,0:T(8,128)(2,1)} %g_hbm.1, f32[64,1024]{1,0:T(8,128)} %f_hbm.1, bf16[128,128]{1,0:T(8,128)(2,1)} %constant.12.clone.outer_hbm, bf16[128,192]{1,0:T(8,128)(2,1)} %constant.13.clone.outer3_hbm, ...), custom_call_target="tpu_custom_call" | custom-call | tf_op jit(solution)/shard_map/pallas_call | solution.py:327
  34.2 0.0 copy-start
  34.2 1.6 %copy.14 = bf16[1,64,1024]{2,1,0:T(8,128)(2,1)} copy(bf16[1,64,1024]{2,1,0:T(8,128)(2,1)} %get-tuple-element.4) | data formatting | bytes 262144
  35.8 0.0 copy-done
  35.8 0.7 %copy.15 = f32[64,1024]{1,0:T(8,128)} copy(f32[64,1024]{1,0:T(8,128)S(1)} %copy-done) | data formatting | bytes 524288
Async XLA Ops:
  34.2 1.6 %copy-start = (f32[64,1024]{1,0:T(8,128)S(1)}, f32[64,1024]{1,0:T(8,128)}, u32[]{:S(2)}) copy-start(f32[64,1024]{1,0:T(8,128)} %get-tuple-element.5) | copy-start | bytes 786436

commit v11 on v9

--- a/solution.py
+++ b/solution.py
@@ -131,11 +131,11 @@
     others = [after(part, step, parts) for step in range(parts)]
 
     def each_other(act):
-        for lead in range(groups):
-            there = after(group, lead, groups)
-
-            for step in range(0 if lead else 1, parts):
-                act(there, others[step])
+        for turn in range(parts):
+            for lead in range(groups):
+                step = (turn + lead * parts // groups) % parts
+                if lead or step:
+                    act(after(group, lead, groups), others[step])
 
     barrier = pltpu.get_barrier_semaphore()
     each_other(

time: 35.3 us -> 35.1 us (level)
  no operation moved by 1% of the time
where the time goes in v11:
time: 35.1 us; the launch traced here: 35 us
  Pallas kernels  32 us (91%)
  local copies, waits for them, and re-layouts  2.32 us (7%)
  between operations  0.65 us (2%)
    pallas_call x1, Pallas kernels, fused_body(): pl.pallas_call(functools.partial(kernel, groups, parts, count, half), out...  32 us
    unnamed x4, local copies, waits for them, and re-layouts  2.32 us

profile of v11, /device:TPU:0, one launch (start us, length us, event | category | flops | bytes accessed | tf_op | source)
XLA Modules:
  0.0 35.0 jit_solution(4670019113900945368)
XLA Ops:
  0.6 32.0 %shard_map.113 = (bf16[1,64,1024]{2,1,0:T(8,128)(2,1)}, f32[64,1024]{1,0:T(8,128)}) custom-call(bf16[1,64,1024]{2,1,0:T(8,128)(2,1)} %x_hbm.1, bf16[1,64,1024]{2,1,0:T(8,128)(2,1)} %g_hbm.1, f32[64,1024]{1,0:T(8,128)} %f_hbm.1, bf16[128,128]{1,0:T(8,128)(2,1)} %constant.12.clone.outer_hbm, bf16[128,192]{1,0:T(8,128)(2,1)} %constant.13.clone.outer3_hbm, ...), custom_call_target="tpu_custom_call" | custom-call | tf_op jit(solution)/shard_map/pallas_call | solution.py:327
  32.6 0.0 copy-start
  32.6 1.6 %copy.14 = bf16[1,64,1024]{2,1,0:T(8,128)(2,1)} copy(bf16[1,64,1024]{2,1,0:T(8,128)(2,1)} %get-tuple-element.4) | data formatting | bytes 262144
  34.2 0.0 copy-done
  34.2 0.7 %copy.15 = f32[64,1024]{1,0:T(8,128)} copy(f32[64,1024]{1,0:T(8,128)S(1)} %copy-done) | data formatting | bytes 524288
Async XLA Ops:
  32.6 1.6 %copy-start = (f32[64,1024]{1,0:T(8,128)S(1)}, f32[64,1024]{1,0:T(8,128)}, u32[]{:S(2)}) copy-start(f32[64,1024]{1,0:T(8,128)} %get-tuple-element.5) | copy-start | bytes 786436
